TPU v7x, 32 devices: a whole 2x2x4 slice. The times are simulated.
32 devices in a mesh: dp: 4 (over x, core), chan: 8 (over z, y).
Axes of the slice: x: 2, y: 2, z: 4, core: 2. Of those that a mesh axis runs over, the one named last changes fastest.
Arguments:
- crop_maps: float32 [8, 128, 3136], P('dp', 'chan'), may hold values from -12 to 12
- out_cotangent: float32 [8, 256, 3136], P('dp', 'chan'), may hold values from -12 to 12
- norm_group: int32 [8], replicated, may hold values from 0 to 3, as said below
- scale_class: int32 [8], replicated, may hold values from 0 to 1
- entry_conv: float32 [256, 9, 128], P('chan'), may hold values from -0.1875 to 0.1875
- middle_conv: float32 [256, 9, 256], P('chan'), may hold values from -0.125 to 0.125
- shortcut_map: float32 [256, 128], P('chan'), may hold values from -0.5 to 0.5
- decoder_conv: float32 [256, 9, 256], P('chan'), may hold values from -0.125 to 0.125
- style_map: float32 [256, 256], P('chan'), may hold values from -3 to 3
- narrow_gain_table: float32 [4, 128], P(None, 'chan'), may hold values from -1 to 1.3
- wide_gain_table: float32 [5, 256], P(None, 'chan'), may hold values from -1 to 1.3
- entry_moment: float32 [256, 9, 128], P('chan'), may hold values from -0.0012207031 to 0.0012207031
- middle_moment: float32 [256, 9, 256], P('chan'), may hold values from -0.0012207031 to 0.0012207031
- shortcut_moment: float32 [256, 128], P('chan'), may hold values from -0.0012207031 to 0.0012207031
- decoder_moment: float32 [256, 9, 256], P('chan'), may hold values from -0.0012207031 to 0.0012207031
- style_moment: float32 [256, 256], P('chan'), may hold values from -0.0012207031 to 0.0012207031
- narrow_moment: float32 [4, 128], P(None, 'chan'), may hold values from -0.0012207031 to 0.0012207031
- wide_moment: float32 [5, 256], P(None, 'chan'), may hold values from -0.0012207031 to 0.0012207031
- entry_square: float32 [256, 9, 128], P('chan'), may hold values from 6.3505934e-10 to 2.5402374e-09
- middle_square: float32 [256, 9, 256], P('chan'), may hold values from 6.3505934e-10 to 2.5402374e-09
- shortcut_square: float32 [256, 128], P('chan'), may hold values from 6.3505934e-10 to 2.5402374e-09
- decoder_square: float32 [256, 9, 256], P('chan'), may hold values from 6.3505934e-10 to 2.5402374e-09
- style_square: float32 [256, 256], P('chan'), may hold values from 6.3505934e-10 to 2.5402374e-09
- narrow_square: float32 [4, 128], P(None, 'chan'), may hold values from 6.3505934e-10 to 2.5402374e-09
- wide_square: float32 [5, 256], P(None, 'chan'), may hold values from 6.3505934e-10 to 2.5402374e-09
Outputs:
- block_out: float32 [8, 256, 3136], P('dp', 'chan')
- input_grad: float32 [8, 128, 3136], P('dp', 'chan')
- entry_weight: float32 [256, 9, 128], P('chan')
- entry_first: float32 [256, 9, 128], P('chan')
- entry_second: float32 [256, 9, 128], P('chan')
- middle_weight: float32 [256, 9, 256], P('chan')
- middle_first: float32 [256, 9, 256], P('chan')
- middle_second: float32 [256, 9, 256], P('chan')
- shortcut_weight: float32 [256, 128], P('chan')
- shortcut_first: float32 [256, 128], P('chan')
- shortcut_second: float32 [256, 128], P('chan')
- decoder_weight: float32 [256, 9, 256], P('chan')
- decoder_first: float32 [256, 9, 256], P('chan')
- decoder_second: float32 [256, 9, 256], P('chan')
- style_weight: float32 [256, 256], P('chan')
- style_first: float32 [256, 256], P('chan')
- style_second: float32 [256, 256], P('chan')
- narrow_weight: float32 [4, 128], P(None, 'chan')
- narrow_first: float32 [4, 128], P(None, 'chan')
- narrow_second: float32 [4, 128], P(None, 'chan')
- wide_weight: float32 [5, 256], P(None, 'chan')
- wide_first: float32 [5, 256], P(None, 'chan')
- wide_second: float32 [5, 256], P(None, 'chan')
- grad_norm: float32 [], replicated
Inputs may be any that keep to these rules, and one draw needn't show every extreme that they name: `norm_group`: each of the 4 groups holds exactly 2 crops.
All inputs are finite; a program needn't handle non-finite values.
Results may differ from a plain program's by a relative error of at most 0.0003.
Values sent between devices are 32-bit elements; how exact they have to be, the bound alone decides.
No kernel may reach another device: no remote copies, remote signals or barrier semaphores. Data moves between devices by JAX's collectives and lax.ppermute only.
A program may use at most 192 MiB of HBM per device.

v0:
```python
import jax
import jax.numpy as jnp
from jax import lax
from jax.sharding import PartitionSpec as P

H_BIG = 56
H_SMALL = 40
NGRP = 4
STEP = 10


beta_one = 0.9
beta_two = 0.999
adam_eps = 1e-08
decay_rate = 0.01
clip_bound = 1.0
norm_eps = 1e-05
style_eps = 1e-06
highest = lax.Precision.HIGHEST
offsets = [(row_step, col_step) for row_step in (-1, 0, 1) for col_step in (-1, 0, 1)]


def shifted(values, row_step, col_step):
    leading = values.shape[0]
    planes = values.shape[1]
    canvas = values.reshape(leading, planes, H_BIG, H_BIG)
    padded = jnp.pad(canvas, ((0, 0), (0, 0), (1, 1), (1, 1)))
    window = padded[:, :, 1 + row_step : 1 + row_step + H_BIG, 1 + col_step : 1 + col_step + H_BIG]
    return window.reshape(leading, planes, H_BIG * H_BIG)


def conv_apply(gathered, weight):
    stacked = jnp.einsum("otc,ncp->ntop", weight, gathered, precision=highest)
    result = shifted(stacked[:, 0], offsets[0][0], offsets[0][1])
    for tap_index in range(1, 9):
        result = result + shifted(
            stacked[:, tap_index], offsets[tap_index][0], offsets[tap_index][1]
        )
    return result


def back_stack(gradient):
    return jnp.stack(
        [shifted(gradient, -offset_pair[0], -offset_pair[1]) for offset_pair in offsets], axis=1
    )


def weight_grad(grad_stack, gathered):
    return jnp.einsum("ntoq,ncq->otc", grad_stack, gathered, precision=highest)


def group_totals_vector(values, group_membership):
    return jnp.dot(group_membership.T, jnp.sum(values, axis=2), precision=highest)


def spread_per_row(table, group_membership):
    return jnp.dot(group_membership, table, precision=highest)[:, :, None]


def silu_slope(values):
    sigmoid_val = jax.nn.sigmoid(values)
    return sigmoid_val * (1.0 + values * (1.0 - sigmoid_val))


def apply_normalization(values, inner_region, group_membership, element_counts):
    totals = lax.psum(group_totals_vector(values * inner_region, group_membership), "dp")
    average = totals / element_counts
    centered = (values - spread_per_row(average, group_membership)) * inner_region
    spread_sum = lax.psum(group_totals_vector(centered * centered, group_membership), "dp")
    variance = spread_sum / element_counts
    scale_per_row = spread_per_row(lax.rsqrt(variance + norm_eps), group_membership)
    return (centered * scale_per_row, scale_per_row)


def normalization_backward(
    partial_results,
    standardized_input,
    scale_per_row,
    group_membership,
    element_counts,
    inner_region,
):
    gradient_portions = []
    for gradient_portion, gain_row in partial_results:
        gradient_portions.append(group_totals_vector(gradient_portion, group_membership))
        gradient_portions.append(
            group_totals_vector(gradient_portion * standardized_input, group_membership)
        )
    totals = lax.psum(jnp.stack(gradient_portions), "dp")
    joined_result = jnp.zeros_like(standardized_input)
    shift_avg = jnp.zeros_like(totals[0])
    average_slope = jnp.zeros_like(totals[0])
    gain_grads = []
    for part_index in range(len(partial_results)):
        gradient_portion = partial_results[part_index][0]
        gain_row = partial_results[part_index][1]
        joined_result = joined_result + gradient_portion * gain_row[None, :, None]
        shift_avg = shift_avg + totals[2 * part_index] * gain_row[None, :]
        average_slope = average_slope + totals[2 * part_index + 1] * gain_row[None, :]
        gain_grads.append(jnp.sum(totals[2 * part_index + 1], axis=0))
        gain_grads.append(jnp.sum(totals[2 * part_index], axis=0))
    result = (
        scale_per_row
        * (
            joined_result
            - spread_per_row(shift_avg / element_counts, group_membership)
            - standardized_input * spread_per_row(average_slope / element_counts, group_membership)
        )
        * inner_region
    )
    return (result, gain_grads)


def conv_back(grad_stack, weight):
    partial_sum = jnp.einsum("otc,ntop->ncp", weight, grad_stack, precision=highest)
    return lax.psum_scatter(partial_sum, "chan", scatter_dimension=1, tiled=True)


def encoder_back(first_stack, hidden_grad, entry_conv, shortcut_map):
    entry_partial = jnp.einsum("otc,ntop->ncp", entry_conv, first_stack, precision=highest)
    shortcut_partial = jnp.einsum("oc,nop->ncp", shortcut_map, hidden_grad, precision=highest)
    return (
        lax.psum_scatter(entry_partial, "chan", scatter_dimension=1, tiled=True),
        lax.psum_scatter(shortcut_partial, "chan", scatter_dimension=1, tiled=True),
    )


def adamw(weight, gradient, moment, square, rate, decay):
    first_new = beta_one * moment + (1.0 - beta_one) * gradient
    second_new = beta_two * square + (1.0 - beta_two) * gradient * gradient
    corrected_first = first_new / (1.0 - beta_one**STEP)
    corrected_second = second_new / (1.0 - beta_two**STEP)
    updated = weight - rate * (
        corrected_first / (jnp.sqrt(corrected_second) + adam_eps) + decay * weight
    )
    return (updated, first_new, second_new)


def body(
    crop_maps,
    out_cotangent,
    norm_group,
    scale_class,
    entry_conv,
    middle_conv,
    shortcut_map,
    decoder_conv,
    style_map,
    narrow_gain_table,
    wide_gain_table,
    entry_moment,
    middle_moment,
    shortcut_moment,
    decoder_moment,
    style_moment,
    narrow_moment,
    wide_moment,
    entry_square,
    middle_square,
    shortcut_square,
    decoder_square,
    style_square,
    narrow_square,
    wide_square,
):
    local_crops = crop_maps.shape[0]
    first_crop = lax.axis_index("dp") * local_crops
    all_member = (norm_group[:, None] == jnp.arange(NGRP, dtype=jnp.int32)[None, :]).astype(
        jnp.float32
    )
    all_pixels = jnp.where(scale_class == 0, H_BIG * H_BIG, H_SMALL * H_SMALL).astype(jnp.float32)
    element_counts = jnp.dot(all_member.T, all_pixels, precision=highest)[:, None]
    group_membership = lax.dynamic_slice_in_dim(all_member, first_crop, local_crops, 0)
    pixels = lax.dynamic_slice_in_dim(all_pixels, first_crop, local_crops, 0)
    classes = lax.dynamic_slice_in_dim(scale_class, first_crop, local_crops, 0)
    positions = jnp.arange(H_BIG * H_BIG, dtype=jnp.int32)
    small_area = ((positions // H_BIG < H_SMALL) & (positions % H_BIG < H_SMALL)).astype(
        jnp.float32
    )
    inner_region = jnp.where(classes[:, None] == 0, 1.0, small_area[None, :])[:, None, :]
    masked_feature_maps = crop_maps * inner_region
    standardized_entry, entry_row_count = apply_normalization(
        masked_feature_maps, inner_region, group_membership, element_counts
    )
    entry_preactivation = (
        standardized_entry * narrow_gain_table[0][None, :, None]
        + narrow_gain_table[1][None, :, None]
    )
    entry_input_map = jax.nn.silu(entry_preactivation) * inner_region
    shortcut_input_map = (
        standardized_entry * narrow_gain_table[2][None, :, None]
        + narrow_gain_table[3][None, :, None]
    ) * inner_region
    whole_entry, whole_shortcut = (
        lax.all_gather(entry_input_map, "chan", axis=1, tiled=True),
        lax.all_gather(shortcut_input_map, "chan", axis=1, tiled=True),
    )
    encoder_block_output = conv_apply(whole_entry, entry_conv)
    shortcut_out = jnp.einsum("oc,ncp->nop", shortcut_map, whole_shortcut, precision=highest)
    standardized_middle, middle_row_count = apply_normalization(
        encoder_block_output, inner_region, group_membership, element_counts
    )
    middle_preactivation = (
        standardized_middle * wide_gain_table[0][None, :, None] + wide_gain_table[1][None, :, None]
    )
    middle_input_map = jax.nn.silu(middle_preactivation) * inner_region
    whole_middle = lax.all_gather(middle_input_map, "chan", axis=1, tiled=True)
    second_out = conv_apply(whole_middle, middle_conv)
    hidden_activation = (shortcut_out + second_out) * inner_region
    pooled = jnp.sum(hidden_activation, axis=2) / pixels[:, None]
    whole_pooled = lax.all_gather(pooled, "chan", axis=1, tiled=True)
    style_scale = lax.rsqrt(jnp.sum(whole_pooled * whole_pooled, axis=1, keepdims=True) + style_eps)
    style_vec = whole_pooled * style_scale
    style_contribution = (
        jnp.dot(style_vec, style_map.T, precision=highest) + wide_gain_table[4][None, :]
    )
    standardized_decoder, decoder_row_count = apply_normalization(
        hidden_activation, inner_region, group_membership, element_counts
    )
    decoder_preactivation = (
        standardized_decoder * wide_gain_table[2][None, :, None]
        + wide_gain_table[3][None, :, None]
        + style_contribution[:, :, None]
    )
    decoder_in = jax.nn.silu(decoder_preactivation) * inner_region
    whole_decoder = lax.all_gather(decoder_in, "chan", axis=1, tiled=True)
    decoder_out = conv_apply(whole_decoder, decoder_conv)
    block_out = (hidden_activation + decoder_out) * inner_region
    top_grad = out_cotangent * inner_region
    top_stack = back_stack(top_grad)
    decoder_wgrad = weight_grad(top_stack, whole_decoder)
    decoder_in_grad = conv_back(top_stack, decoder_conv)
    decoder_preactivation_grad = decoder_in_grad * silu_slope(decoder_preactivation) * inner_region
    style_grad = jnp.sum(decoder_preactivation_grad, axis=2)
    style_wgrad = jnp.dot(style_grad.T, style_vec, precision=highest)
    style_bias_grad = jnp.sum(style_grad, axis=0)
    style_vec_grad = lax.psum(jnp.dot(style_grad, style_map, precision=highest), "chan")
    pooled_grad = style_scale * (
        style_vec_grad - style_vec * jnp.sum(style_vec_grad * style_vec, axis=1, keepdims=True)
    )
    own_channels = pooled.shape[1]
    own_pooled_grad = lax.dynamic_slice_in_dim(
        pooled_grad, lax.axis_index("chan") * own_channels, own_channels, 1
    )
    decoder_norm_grad, decoder_gain_grads = normalization_backward(
        [(decoder_preactivation_grad, wide_gain_table[2])],
        standardized_decoder,
        decoder_row_count,
        group_membership,
        element_counts,
        inner_region,
    )
    hidden_grad = (
        top_grad
        + decoder_norm_grad
        + (own_pooled_grad / pixels[:, None])[:, :, None] * inner_region
    )
    hidden_stack = back_stack(hidden_grad)
    middle_wgrad = weight_grad(hidden_stack, whole_middle)
    shortcut_wgrad = jnp.einsum("nop,ncp->oc", hidden_grad, whole_shortcut, precision=highest)
    middle_in_grad = conv_back(hidden_stack, middle_conv)
    middle_preactivation_grad = middle_in_grad * silu_slope(middle_preactivation) * inner_region
    first_grad, middle_gain_grads = normalization_backward(
        [(middle_preactivation_grad, wide_gain_table[0])],
        standardized_middle,
        middle_row_count,
        group_membership,
        element_counts,
        inner_region,
    )
    first_stack = back_stack(first_grad)
    entry_wgrad = weight_grad(first_stack, whole_entry)
    entry_in_grad, shortcut_in_grad = encoder_back(
        first_stack, hidden_grad, entry_conv, shortcut_map
    )
    entry_pre_grad = entry_in_grad * silu_slope(entry_preactivation) * inner_region
    shortcut_pre_grad = shortcut_in_grad * inner_region
    maps_grad, narrow_grads = normalization_backward(
        [(entry_pre_grad, narrow_gain_table[0]), (shortcut_pre_grad, narrow_gain_table[2])],
        standardized_entry,
        entry_row_count,
        group_membership,
        element_counts,
        inner_region,
    )
    entry_sum, middle_sum, shortcut_sum, decoder_sum, style_sum, style_bias_sum = lax.psum(
        (entry_wgrad, middle_wgrad, shortcut_wgrad, decoder_wgrad, style_wgrad, style_bias_grad),
        "dp",
    )
    narrow_grad = jnp.stack(narrow_grads)
    wide_grad = jnp.stack(
        [
            middle_gain_grads[0],
            middle_gain_grads[1],
            decoder_gain_grads[0],
            decoder_gain_grads[1],
            style_bias_sum,
        ]
    )
    gradients = (
        entry_sum,
        middle_sum,
        shortcut_sum,
        decoder_sum,
        style_sum,
        narrow_grad,
        wide_grad,
    )
    local_squares = jnp.zeros((), jnp.float32)
    for gradient in gradients:
        local_squares = local_squares + jnp.sum(gradient * gradient)
    total_squares = lax.psum(local_squares, "chan")
    grad_norm = jnp.sqrt(total_squares)
    clip_factor = jnp.minimum(1.0, clip_bound / grad_norm)
    params = (
        entry_conv,
        middle_conv,
        shortcut_map,
        decoder_conv,
        style_map,
        narrow_gain_table,
        wide_gain_table,
    )
    moments = (
        entry_moment,
        middle_moment,
        shortcut_moment,
        decoder_moment,
        style_moment,
        narrow_moment,
        wide_moment,
    )
    squares = (
        entry_square,
        middle_square,
        shortcut_square,
        decoder_square,
        style_square,
        narrow_square,
        wide_square,
    )
    rates = (0.06, 0.04, 0.16, 0.04, 1.0, 0.4, 0.4)
    decays = (decay_rate, decay_rate, decay_rate, decay_rate, decay_rate, 0.0, 0.0)
    results = [block_out, maps_grad * inner_region]
    for which in range(7):
        updated, first_new, second_new = adamw(
            params[which],
            gradients[which] * clip_factor,
            moments[which],
            squares[which],
            rates[which],
            decays[which],
        )
        results.append(updated)
        results.append(first_new)
        results.append(second_new)
    return (
        results[0],
        results[1],
        results[2],
        results[3],
        results[4],
        results[5],
        results[6],
        results[7],
        results[8],
        results[9],
        results[10],
        results[11],
        results[12],
        results[13],
        results[14],
        results[15],
        results[16],
        results[17],
        results[18],
        results[19],
        results[20],
        results[21],
        results[22],
        grad_norm,
    )


def solution(mesh):
    return jax.shard_map(
        body,
        mesh=mesh,
        in_specs=(
            P("dp", "chan", None),
            P("dp", "chan", None),
            P(),
            P(),
            P("chan", None, None),
            P("chan", None, None),
            P("chan", None),
            P("chan", None, None),
            P("chan", None),
            P(None, "chan"),
            P(None, "chan"),
            P("chan", None, None),
            P("chan", None, None),
            P("chan", None),
            P("chan", None, None),
            P("chan", None),
            P(None, "chan"),
            P(None, "chan"),
            P("chan", None, None),
            P("chan", None, None),
            P("chan", None),
            P("chan", None, None),
            P("chan", None),
            P(None, "chan"),
            P(None, "chan"),
        ),
        out_specs=(
            P("dp", "chan", None),
            P("dp", "chan", None),
            P("chan", None, None),
            P("chan", None, None),
            P("chan", None, None),
            P("chan", None, None),
            P("chan", None, None),
            P("chan", None, None),
            P("chan", None),
            P("chan", None),
            P("chan", None),
            P("chan", None, None),
            P("chan", None, None),
            P("chan", None, None),
            P("chan", None),
            P("chan", None),
            P("chan", None),
            P(None, "chan"),
            P(None, "chan"),
            P(None, "chan"),
            P(None, "chan"),
            P(None, "chan"),
            P(None, "chan"),
            P(),
        ),
        check_vma=False,
    )
```

profile of v0, /device:TPU:0, one launch (start us, length us, event | category | flops | bytes accessed | tf_op | source)
XLA Modules:
  0.0 1129.6 jit_solution(3629393786552800123)
XLA Ops:
  11.8 8.3 psum.119
  30.1 62.4 %all-gather.8.cloned.1.call-done = f32[2,128,3136]{2,1,0:T(8,128)} async-done(((f32[2,16,3136]{2,1,0:T(8,128)}), f32[2,128,3136]{2,1,0:T(8,128)}) %all-gather.8.cloned.1.call-update) | async-done | bytes 3211280 | tf_op jit(solution)/shard_map/all_gather | solution.py:195
  128.8 14.1 %multiply_reduce_fusion.1 = (f32[2,32]{1,0:T(2,128)S(1)}, f32[2,32,56,56]{3,2,1,0:T(8,128)}, f32[2,32,56,56]{3,2,1,0:T(8,128)}, f32[2,32,56,56]{3,2,1,0:T(8,128)...) fusion(f32[2,56,56]{2,1,0:T(8,128)S(1)} %broadcast_select_fusion, ...), kind=kLoop, calls=%fused_computation.77 | loop fusion | flops 2006976 | bytes 12067584 | tf_op jit(solution)/shard_map/reduce_sum | solution.py:53
  178.4 13.1 %pad_slice_fusion.16 = (f32[2,32,56,56]{3,2,1,0:T(8,128)}, f32[2,32,56,56]{3,2,1,0:T(8,128)}, f32[2,32,56,56]{3,2,1,0:T(8,128)}, f32[2,32,56,56]{3,2,1,0:T(8,128...) fusion(f32[2,32,56,56]{3,2,1,0:T(8,128)} %reshape.263), kind=kLoop, calls=%fused_computation.35 | loop fusion | bytes 7225344 | tf_op jit(solution)/shard_map/slice | solution.py:28
  219.8 14.2 %convolution_bitcast_fusion.4 = f32[2,256,3136]{2,1,0:T(8,128)} fusion(f32[2,9,32,3136]{3,2,0,1:T(8,128)S(1)} %constant_dynamic-update-slice_fusion, f32[32,9,256]{2,0,1:T(8,128)S(1)} %copy-done.26), kind=kOutput, calls=%fused_computation.10 | convolution fusion | flops 5549064192 | bytes 13942784 | tf_op jit(solution)/shard_map/otc,ntop->ncp/dot_general | solution.py:115
  234.8 41.2 %all-gather.10.cloned.1.call-done = f32[2,256,3136]{2,1,0:T(8,128)} async-done(((f32[2,32,3136]{2,1,0:T(8,128)}), f32[2,256,3136]{2,1,0:T(8,128)}) %all-gather.10.cloned.1.call-update) | async-done | bytes 6422544 | tf_op jit(solution)/shard_map/all_gather | solution.py:207
  276.1 9.5 convolution_bitcast_fusion.1
  358.0 19.1 %all-gather = f32[8,32,2]{1,2,0:T(2,128)S(1)} all-gather(f32[1,32,2]{1,2,0:T(2,128)S(1)} %divide_bitcast_fusion), channel_id=1, replica_groups=mesh['dp'=4,'chan'=8] {'chan'}, dimensions={0}, use_global_device_ids=true | all-gather | bytes 2304 | tf_op jit(solution)/shard_map/all_gather | solution.py:211
  384.0 78.3 %reduce-scatter.5.cloned.1.call-done = f32[2,32,3136]{2,1,0:T(8,128)} async-done(((f32[2,256,3136]{2,1,0:T(8,128)}), f32[2,32,3136]{2,1,0:T(8,128)}) %reduce-scatter.5.cloned.1.call-update) | async-done | bytes 802832 | tf_op jit(solution)/shard_map/reduce_scatter | solution.py:116
  466.2 20.0 %psum.126 = f32[2,256]{1,0:T(2,128)S(1)} all-reduce(f32[2,256]{1,0:T(2,128)S(1)} %fusion.189), channel_id=1, replica_groups=mesh['dp'=4,'chan'=8] {'chan'}, use_global_device_ids=true, to_apply=%region_18.19 | all-reduce | flops 512 | bytes 4096 | tf_op jit(solution)/shard_map/psum | solution.py:237
  493.3 74.4 %all-gather.12.cloned.1.call-done = f32[2,256,3136]{2,1,0:T(8,128)} async-done(((f32[2,32,3136]{2,1,0:T(8,128)}), f32[2,256,3136]{2,1,0:T(8,128)}) %all-gather.12.cloned.1.call-update) | async-done | bytes 6422544 | tf_op jit(solution)/shard_map/all_gather | solution.py:226
  567.7 9.6 convolution_bitcast_fusion
  645.0 13.0 %pad_slice_fusion.8 = (f32[2,32,56,56]{3,2,1,0:T(8,128)}, f32[2,32,56,56]{3,2,1,0:T(8,128)}, f32[2,32,56,56]{3,2,1,0:T(8,128)}, f32[2,32,56,56]{3,2,1,0:T(8,128)...) fusion(f32[2,32,56,56]{3,2,1,0:T(8,128)} %reshape.264), kind=kLoop, calls=%fused_computation.27 | loop fusion | bytes 7225344 | tf_op jit(solution)/shard_map/slice | solution.py:28
  686.8 14.1 %convolution_bitcast_fusion.3 = f32[2,256,3136]{2,1,0:T(8,128)} fusion(f32[2,9,32,3136]{3,2,0,1:T(8,128)S(1)} %constant_dynamic-update-slice_fusion.8, f32[32,9,256]{2,0,1:T(8,128)S(1)} %copy-done.24), kind=kOutput, calls=%fused_computation.9 | convolution fusion | flops 5549064192 | bytes 13942784 | tf_op jit(solution)/shard_map/otc,ntop->ncp/dot_general | solution.py:115
  701.0 18.4 %fusion.23 = f32[32,9,256]{2,0,1:T(8,128)} fusion(f32[2,9,32,3136]{3,2,0,1:T(8,128)} %copy-done.1, f32[2,256,3136]{2,1,0:T(8,128)} %all-gather.12.cloned.1.call-done), kind=kOutput, calls=%fused_computation.80 | convolution fusion | flops 5549064192 | bytes 13942784 | tf_op jit(solution)/shard_map/ntoq,ncq->otc/dot_general | solution.py:49
  719.4 9.4 fusion.20
  728.8 92.1 %reduce-scatter.7.cloned.1.call-done = f32[2,32,3136]{2,1,0:T(8,128)} async-done(((f32[2,256,3136]{2,1,0:T(8,128)}), f32[2,32,3136]{2,1,0:T(8,128)}) %reduce-scatter.7.cloned.1.call-update) | async-done | bytes 802832 | tf_op jit(solution)/shard_map/reduce_scatter | solution.py:116
  831.5 13.0 %pad_slice_fusion = (f32[2,32,56,56]{3,2,1,0:T(8,128)}, f32[2,32,56,56]{3,2,1,0:T(8,128)}, f32[2,32,56,56]{3,2,1,0:T(8,128)}, f32[2,32,56,56]{3,2,1,0:T(8,128)},...) fusion(f32[2,32,56,56]{3,2,1,0:T(8,128)} %reshape.265), kind=kLoop, calls=%fused_computation.19 | loop fusion | bytes 7225344 | tf_op jit(solution)/shard_map/slice | solution.py:28
  886.1 10.2 convolution_bitcast_fusion.6
  902.8 11.7 %all-reduce.31.cloned.1.call-done = (f32[32,9,128]{2,0,1:T(8,128)}, f32[32,9,256]{2,0,1:T(8,128)}, f32[32,9,256]{2,0,1:T(8,128)}) async-done(((f32[32,9,128]{2,0,1:T(8,128)}, f32[32,9,256]{2,0,1:T(8,128)}, f32[32,9,256]{2,0,1:T(8,128)}), (f32[32,9,128]{2,0,1:T(8,128)}, f32[32,9,256]{2,0,1:T(8,128)}, f32[32,9,256]{2,0,1:T(8,128)})) %all-reduce.31.cloned.1.call-update) | async-done | bytes 737296 | tf_op jit(solution)/shard_map/psum | solution.py:286
  920.7 74.0 %reduce-scatter.11.cloned.1.call-done = f32[2,16,3136]{2,1,0:T(8,128)} async-done(((f32[2,128,3136]{2,1,0:T(8,128)}), f32[2,16,3136]{2,1,0:T(8,128)}) %reduce-scatter.11.cloned.1.call-update) | async-done | bytes 401424 | tf_op jit(solution)/shard_map/reduce_scatter | solution.py:124
  994.7 79.2 %reduce-scatter.9.cloned.1.call-done = f32[2,16,3136]{2,1,0:T(8,128)} async-done(((f32[2,128,3136]{2,1,0:T(8,128)}), f32[2,16,3136]{2,1,0:T(8,128)}) %reduce-scatter.9.cloned.1.call-update) | async-done | bytes 401424 | tf_op jit(solution)/shard_map/reduce_scatter | solution.py:123
  1076.2 11.2 all-reduce.27
  1093.5 20.0 %psum.135 = f32[]{:T(128)} all-reduce(f32[]{:T(128)S(6)} %add.554), channel_id=1, replica_groups=mesh['dp'=4,'chan'=8] {'chan'}, use_global_device_ids=true, to_apply=%region_53.54 | all-reduce | flops 1 | bytes 8 | tf_op jit(solution)/shard_map/psum | solution.py:312
  (374 shorter events, 377.1 us)
Async XLA Ops:
  7.2 85.3 %all-gather.8.cloned.1.call-start = ((), (), s32[]{:S(2)}) async-start(), calls=%async_computation.5 | async-start | bytes 3686400 | tf_op jit(solution)/shard_map/all_gather | solution.py:195
  8.8 820.1 %copy-start.76 = (f32[4]{0:T(128)}, f32[4]{0:T(128)S(1)}, u32[]{:S(2)}) copy-start(f32[4]{0:T(128)S(1)} %convolution_bitcast_fusion.17) | copy-start | bytes 52
  9.6 819.3 %copy-start.74 = (pred[2,4]{1,0:T(4,128)(4,1)}, pred[2,4]{1,0:T(4,128)(4,1)S(1)}, u32[]{:S(2)}) copy-start(pred[2,4]{1,0:T(4,128)(4,1)S(1)} %constant_dynamic-slice_fusion) | copy-start | bytes 28
  29.9 246.2 %all-gather.10.cloned.1.call-start = ((), (), s32[]{:S(2)}) async-start(), calls=%async_computation.6 | async-start | bytes 7372800 | tf_op jit(solution)/shard_map/all_gather | solution.py:207
  175.5 169.7 %all-gather.6.cloned.1.call-start = ((), (), s32[]{:S(2)}) async-start(), calls=%async_computation.4 | async-start | bytes 3686400 | tf_op jit(solution)/shard_map/all_gather | solution.py:196
  176.2 286.1 %reduce-scatter.5.cloned.1.call-start = ((), (), s32[]{:S(2)}) async-start(), calls=%async_computation.8 | async-start | bytes 7372800 | tf_op jit(solution)/shard_map/reduce_scatter | solution.py:116
  234.1 333.6 %all-gather.12.cloned.1.call-start = ((), (), s32[]{:S(2)}) async-start(), calls=%async_computation.7 | async-start | bytes 7372800 | tf_op jit(solution)/shard_map/all_gather | solution.py:226
  466.0 354.8 %reduce-scatter.7.cloned.1.call-start = ((), (), s32[]{:S(2)}) async-start(), calls=%async_computation.9 | async-start | bytes 7372800 | tf_op jit(solution)/shard_map/reduce_scatter | solution.py:116
  700.9 213.6 %all-reduce.31.cloned.1.call-start = ((), (), s32[]{:S(2)}) async-start(), calls=%async_computation.12 | async-start | bytes 1474560 | tf_op jit(solution)/shard_map/psum | solution.py:286
  880.6 114.1 %reduce-scatter.11.cloned.1.call-start = ((), (), s32[]{:S(2)}) async-start(), calls=%async_computation.11 | async-start | bytes 3686400 | tf_op jit(solution)/shard_map/reduce_scatter | solution.py:124
  885.2 188.7 %reduce-scatter.9.cloned.1.call-start = ((), (), s32[]{:S(2)}) async-start(), calls=%async_computation.10 | async-start | bytes 3686400 | tf_op jit(solution)/shard_map/reduce_scatter | solution.py:123
  902.6 212.3 %copy-start.52 = (f32[5,32]{1,0:T(8,128)S(1)}, f32[5,32]{1,0:T(8,128)}, u32[]{:S(2)}) copy-start(f32[5,32]{1,0:T(8,128)} %param.35) | copy-start | bytes 1924
  902.6 212.3 %copy-start.66 = (f32[5,32]{1,0:T(8,128)S(1)}, f32[5,32]{1,0:T(8,128)}, u32[]{:S(2)}) copy-start(f32[5,32]{1,0:T(8,128)} %param.42) | copy-start | bytes 1924
  902.6 212.3 %copy-start.67 = (f32[5,32]{1,0:T(8,128)S(1)}, f32[5,32]{1,0:T(8,128)}, u32[]{:S(2)}) copy-start(f32[5,32]{1,0:T(8,128)} %param.49) | copy-start | bytes 1924
  902.7 212.9 %copy-start.43 = (f32[32,128]{1,0:T(8,128)S(1)}, f32[32,128]{1,0:T(8,128)}, u32[]{:S(2)}) copy-start(f32[32,128]{1,0:T(8,128)} %param.38) | copy-start | bytes 49156
  902.7 212.9 %copy-start.44 = (f32[32,128]{1,0:T(8,128)S(1)}, f32[32,128]{1,0:T(8,128)}, u32[]{:S(2)}) copy-start(f32[32,128]{1,0:T(8,128)} %param.45) | copy-start | bytes 49156
  902.7 213.5 %copy-start.41 = (f32[32,256]{1,0:T(8,128)S(1)}, f32[32,256]{1,0:T(8,128)}, u32[]{:S(2)}) copy-start(f32[32,256]{1,0:T(8,128)} %param.40) | copy-start | bytes 98308
  902.7 213.5 %copy-start.42 = (f32[32,256]{1,0:T(8,128)S(1)}, f32[32,256]{1,0:T(8,128)}, u32[]{:S(2)}) copy-start(f32[32,256]{1,0:T(8,128)} %param.47) | copy-start | bytes 98308
  902.7 214.2 %copy-start.38 = (f32[32,9,128]{2,0,1:T(8,128)S(1)}, f32[32,9,128]{2,0,1:T(8,128)}, u32[]{:S(2)}) copy-start(f32[32,9,128]{2,0,1:T(8,128)} %param.36) | copy-start | bytes 442372
  902.7 214.2 %copy-start.39 = (f32[32,9,128]{2,0,1:T(8,128)S(1)}, f32[32,9,128]{2,0,1:T(8,128)}, u32[]{:S(2)}) copy-start(f32[32,9,128]{2,0,1:T(8,128)} %param.43) | copy-start | bytes 442372
  902.7 215.0 %copy-start.25 = (f32[32,9,256]{2,0,1:T(8,128)S(1)}, f32[32,9,256]{2,0,1:T(8,128)}, u32[]{:S(2)}) copy-start(f32[32,9,256]{2,0,1:T(8,128)} %param.30) | copy-start | bytes 884740
  902.8 215.0 %copy-start.28 = (f32[32,9,256]{2,0,1:T(8,128)S(1)}, f32[32,9,256]{2,0,1:T(8,128)}, u32[]{:S(2)}) copy-start(f32[32,9,256]{2,0,1:T(8,128)} %param.32) | copy-start | bytes 884740
  902.8 215.0 %copy-start.35 = (f32[32,9,256]{2,0,1:T(8,128)S(1)}, f32[32,9,256]{2,0,1:T(8,128)}, u32[]{:S(2)}) copy-start(f32[32,9,256]{2,0,1:T(8,128)} %param.39) | copy-start | bytes 884740
  902.8 214.9 %copy-start.36 = (f32[32,9,256]{2,0,1:T(8,128)S(1)}, f32[32,9,256]{2,0,1:T(8,128)}, u32[]{:S(2)}) copy-start(f32[32,9,256]{2,0,1:T(8,128)} %param.46) | copy-start | bytes 884740
  (63 other events, 3794.2 us)
Sparse Core Ops, SparseCore 0:
  30.0 62.4 all-gather.7
  175.6 100.4 all-gather.9
  278.3 60.1 all-gather.5
  341.9 120.3 reduce-scatter.4
  466.2 101.4 all-gather.11
  701.0 119.8 reduce-scatter.6
  880.7 33.7 all-reduce.30
  918.1 76.5 reduce-scatter.10
  998.7 75.0 reduce-scatter.8
where the time goes:
time: 1140 us; the launch traced here: 1130 us
  waiting for transfers between devices  514 us (45%)
  local copies, waits for them, and re-layouts  285 us (25%)
  matrix products  122 us (11%)
  blocking collectives  121 us (11%)
  other arithmetic  65 us (6%)
  between operations  21.8 us (2%)
    reduce_scatter x2, waiting for transfers between devices, conv_back(): lax.psum_scatter(partial_sum, 'chan', scatter_dimension=1, tiled=True)  170 us
    reduce_scatter x1, waiting for transfers between devices, encoder_back(): lax.psum_scatter(entry_partial, 'chan', scatter_dimension=1, tiled=True)  79.2 us
    all_gather x1, waiting for transfers between devices, body(): whole_decoder = lax.all_gather(decoder_in, 'chan', axis=1, tiled=True)  74.4 us
    reduce_scatter x1, waiting for transfers between devices, encoder_back(): lax.psum_scatter(shortcut_partial, 'chan', scatter_dimension=1, tiled=True)  74 us
    another operation x24, local copies, waits for them, and re-layouts, shifted(): canvas = values.reshape(leading, planes, H_BIG, H_BIG)  68.6 us
    slice x11, local copies, waits for them, and re-layouts, shifted(): padded[:, :, 1 + row_step:1 + row_step + H_BIG, 1 + col_step:1 + col_step...  64.7 us
    another operation x27, local copies, waits for them, and re-layouts, back_stack(): jnp.stack([shifted(gradient, -offset_pair[0], -offset_pair[1]) for offset...  64.4 us
    all_gather x1, waiting for transfers between devices, body(): lax.all_gather(entry_input_map, 'chan', axis=1, tiled=True)  62.4 us
  transfers between devices with their start and end apart: 9, of which 8 were waited for; matrix products, arithmetic and copies ran while one was open for 16% of the time, Pallas kernels for 0%

commit v1 on v0

v1 whole, which is shorter than its diff:
```python
import functools

import jax
import jax.numpy as jnp
from jax import lax
from jax.experimental import pallas as pl
from jax.experimental.pallas import tpu as pltpu
from jax.sharding import PartitionSpec as P

SIDE = 56
H_SMALL = 40
NGRP = 4
STEP = 10
TAPS = 9

beta_one = 0.9
beta_two = 0.999
adam_eps = 1e-08
decay_rate = 0.01
clip_bound = 1.0
norm_eps = 1e-05
style_eps = 1e-06
highest = lax.Precision.HIGHEST
BOTH = ("dp", "chan")
f32, bf16 = jnp.float32, jnp.bfloat16
SMEM = pl.BlockSpec(memory_space=pltpu.SMEM)
VMEM = pl.BlockSpec(memory_space=pltpu.VMEM)
NN = (((1,), (0,)), ((), ()))
NT = (((1,), (1,)), ((), ()))


def gray(number):
    return number ^ (number >> 1)


def pair_bits(bits):
    stages = []
    for start in range(0, len(bits), 2):
        pair = bits[start : start + 2]
        stages.append([pair[0]] if len(pair) == 1 else [pair[0], pair[1], pair[0] ^ pair[1]])
    return stages


class Plan:
    def __init__(self, mesh, crop_shape, out_shape):
        self.n_dp, self.n_chan = mesh.shape["dp"], mesh.shape["chan"]
        self.n_all = self.n_dp * self.n_chan
        self.held, self.in_own = crop_shape[0], crop_shape[1]
        self.out_own = out_shape[1]
        self.n_in, self.n_out = self.in_own * self.n_chan, self.out_own * self.n_chan
        self.n_crops = self.held * self.n_dp
        self.strips = self.n_chan // self.held
        self.rows = -(-SIDE // self.strips)
        self.cells, self.cells_halo = self.rows * SIDE, (self.rows + 2) * SIDE
        self.strip_of = [0] * self.strips
        for strip in range(self.strips):
            self.strip_of[gray(strip)] = strip
        self.parts = 2 if (self.out_own // 2) % 8 == 0 else 1
        self.part = self.out_own // self.parts
        self.core_mask = self.n_chan
        self.strip_bits = [1 << k for k in range(self.strips.bit_length() - 1)]
        self.crop_bits = [1 << k for k in range(self.n_chan.bit_length() - 1) if (1 << k) >= self.strips]
        self.chan_bits = self.strip_bits + self.crop_bits
        self.far_bits = [self.n_chan << k for k in range(1, self.n_dp.bit_length() - 1)]
        self.dp_bits = [1 << k for k in range(self.n_dp.bit_length() - 1)]
        self.quick = self.strips == 4


def swap(block, mask, plan):
    return lax.ppermute(block, BOTH, [(i, i ^ mask) for i in range(plan.n_all)])


def split(values):
    top = values.astype(bf16)
    return top, (values - top.astype(f32)).astype(bf16)


def dot3(left, right, dims):
    (left_top, left_low), (right_top, right_low) = left, right
    dot = functools.partial(lax.dot_general, dimension_numbers=dims, preferred_element_type=f32)
    return dot(left_top, right_top) + dot(left_low, right_top) + dot(left_top, right_low)


def device_at():
    return lax.axis_index("dp"), lax.axis_index("chan")


def crop_strip(plan, dp_at, chan_at):
    low = chan_at & (plan.strips - 1)
    strip = low
    for k in range(1, plan.strips.bit_length() - 1):
        strip = strip ^ (low >> k)
    return dp_at * plan.held + chan_at // plan.strips, strip


def side_of(class_ref, crop):
    return jnp.where(class_ref[crop] == 0, SIDE, H_SMALL)


def group_cells(plan, group_ref, class_ref, crop):
    total = jnp.int32(0)
    for other in range(plan.n_crops):
        side = side_of(class_ref, other)
        total = total + jnp.where(group_ref[other] == group_ref[crop], side * side, 0)
    return total.astype(f32)


def inside_mask(plan, class_ref, crop, strip, columns, halo):
    side = side_of(class_ref, crop)
    col = lax.broadcasted_iota(jnp.int32, (SIDE, columns), 0)
    in_cols = jnp.where(col < side, 1.0, 0.0).astype(f32)
    rows = range(-1, plan.rows + 1) if halo else range(plan.rows)
    pieces = []
    for row in rows:
        at = strip * plan.rows + row
        pieces.append(in_cols * jnp.where((at >= 0) & (at < side), 1.0, 0.0).astype(f32))
    return jnp.concatenate(pieces, axis=0)


def shifted_columns(values):
    length = values.shape[0]
    col = lax.broadcasted_iota(jnp.int32, values.shape, 0) % SIDE
    left = jnp.where(col == 0, 0.0, jnp.roll(values, 1, 0))
    right = jnp.where(col == SIDE - 1, 0.0, jnp.roll(values, -1, 0))
    return left, values, right


def fill_taps(plan, values, even, odd):
    for b, moved in enumerate(shifted_columns(values)):
        top, low = split(moved)
        even[0, b], even[1, b] = top, low
        top, low = split(moved[SIDE : SIDE + plan.cells])
        odd[0, b], odd[1, b] = top, low


def read_tap(plan, even, odd, a, b):
    if a == 1:
        return odd[0, b], odd[1, b]
    start = 2 * SIDE if a == 2 else 0
    return even[0, b, start : start + plan.cells], even[1, b, start : start + plan.cells]


def tap_scratch(plan, columns):
    return [
        pltpu.VMEM((2, 3, plan.cells_halo, columns), bf16),
        pltpu.VMEM((2, 3, plan.cells, columns), bf16),
    ]


def fill_weight(plan, masks, refs, weight):
    dp_at, chan_at = device_at()
    for q, ref in enumerate(refs):
        part_at = ((dp_at & 1) ^ q) * plan.part if plan.parts > 1 else 0
        for j, mask in enumerate(masks):
            first = pl.multiple_of((chan_at ^ mask) * plan.out_own + part_at, 8)
            for t in range(TAPS):
                weight[t, pl.ds(first, plan.part), :] = ref[j, t * plan.part : (t + 1) * plan.part, :]


def fill_flat(plan, masks, refs, start, flat):
    dp_at, chan_at = device_at()
    for q, ref in enumerate(refs):
        part_at = ((dp_at & 1) ^ q) * plan.part if plan.parts > 1 else 0
        for j, mask in enumerate(masks):
            first = pl.multiple_of((chan_at ^ mask) * plan.out_own + part_at, 8)
            flat[pl.ds(first, plan.part), :] = ref[j, start : start + plan.part, :]


def conv_forward(plan, even, odd, weight):
    total = None
    for a in range(3):
        for b in range(3):
            term = dot3(read_tap(plan, even, odd, a, b), split(weight[3 * a + b]), NT)
            total = term if total is None else total + term
    return total


def conv_backward(plan, even, odd, weight):
    total = None
    for a in range(3):
        for b in range(3):
            term = dot3(read_tap(plan, even, odd, 2 - a, 2 - b), split(weight[3 * a + b]), NN)
            total = term if total is None else total + term
    return total


def row_sum(values):
    return jnp.sum(values, axis=0, keepdims=True)


def tile(rows, columns):
    blank = jnp.zeros((8 - len(rows), columns), f32)
    return jnp.concatenate(list(rows) + [blank], axis=0)


def local_stats(plan, class_ref, crop, strip, values, inside):
    side = side_of(class_ref, crop)
    cells = (jnp.clip(side - strip * plan.rows, 0, plan.rows) * side).astype(f32)
    mean = row_sum(values * inside) / jnp.maximum(cells, 1.0)
    centered = (values - mean) * inside
    return tile([mean, row_sum(centered * centered)], values.shape[1])


def write_messages(strip, stats, values, messages):
    alone, with_a, with_b = messages
    alone[...] = stats
    first, last = values[:SIDE], values[-SIDE:]
    with_a[:8] = stats
    with_b[:8] = stats
    with_a[8:] = jnp.where((strip & 1) == 0, last, first)
    with_b[8:] = jnp.where(strip == 1, last, first)


def with_edges(plan, strip, values, edge_a, edge_b):
    a, b = edge_a[8:], edge_b[8:]
    if plan.quick:
        a_above = (strip & 1) == 1
        above, below = jnp.where(a_above, a, b), jnp.where(a_above, b, a)
    else:
        above, below = a, b
    return jnp.concatenate([above, values, below], axis=0)


def crop_entries(plan, refs, masks):
    dp_at, chan_at = device_at()
    me = dp_at * plan.n_chan + chan_at
    entries, k = [], 0
    for ref in refs:
        for at in range(ref.shape[0] // 8):
            other = me ^ masks[k]
            crop, _ = crop_strip(plan, other // plan.n_chan, other % plan.n_chan)
            entries.append((crop, ref[8 * at : 8 * at + 8]))
            k += 1
    return entries


def group_stats(plan, group_ref, class_ref, crop, entries):
    count = group_cells(plan, group_ref, class_ref, crop)
    weights, mean = [], 0.0
    for other, block in entries:
        side = side_of(class_ref, other)
        same = jnp.where(group_ref[other] == group_ref[crop], 1.0, 0.0).astype(f32)
        cells = (side * side).astype(f32)
        weights.append((same, same * cells))
        mean = mean + (same * cells) * block[0:1]
    mean = mean / count
    total = 0.0
    for (same, cells), (other, block) in zip(weights, entries):
        spread = block[0:1] - mean
        total = total + same * block[1:2] + cells * (spread * spread)
    return mean, lax.rsqrt(total / count + norm_eps)


def group_sums(plan, group_ref, crop, entries, n_rows):
    total = 0.0
    for other, block in entries:
        total = total + jnp.where(group_ref[other] == group_ref[crop], 1.0, 0.0).astype(f32) * block[0:n_rows]
    return total


def sigmoid(values):
    return 1.0 / (1.0 + jnp.exp(-values))


def silu(values):
    return values * sigmoid(values)


def silu_slope(values):
    sig = sigmoid(values)
    return sig * (1.0 + values * (1.0 - sig))


def crop_inside(plan, class_ref, dp_at, which, shape):
    side = side_of(class_ref, dp_at * plan.held + which)
    at = lax.broadcasted_iota(jnp.int32, shape, 1)
    row = at // SIDE
    return jnp.where((row < side) & (at - row * SIDE < side), 1.0, 0.0).astype(f32)


def stats_kernel(plan, class_ref, maps, out):
    dp_at, _ = device_at()
    for which in range(plan.held):
        inside = crop_inside(plan, class_ref, dp_at, which, maps.shape[1:])
        side = side_of(class_ref, dp_at * plan.held + which)
        cells = (side * side).astype(f32)
        values = maps[which] * inside
        mean = jnp.sum(values, axis=1, keepdims=True) / cells
        centered = (values - mean) * inside
        squares = jnp.sum(centered * centered, axis=1, keepdims=True)
        out[0, which] = jnp.broadcast_to(mean, (plan.in_own, 128))
        out[1, which] = jnp.broadcast_to(squares, (plan.in_own, 128))


def pack_strips(plan, values, which, send):
    blank = jnp.zeros((values.shape[0], SIDE), f32)
    tail = plan.strips * plan.rows - SIDE + 1
    padded = jnp.concatenate([blank, values] + [blank] * tail, axis=1)
    for strip in range(plan.strips):
        first = strip * plan.cells
        send[which * plan.strips + gray(strip)] = padded[:, first : first + plan.cells_halo]


def norm_kernel(plan, masks, group_ref, class_ref, maps, *refs):
    parts, (norm, scales, send) = refs[:-3], refs[-3:]
    dp_at, _ = device_at()
    entries, k = [], 0
    for ref in parts:
        for block in range(ref.shape[0] // 2):
            for which in range(plan.held):
                entries.append(((dp_at ^ masks[k]) * plan.held + which, ref, block, which))
            k += 1
    for which in range(plan.held):
        crop = dp_at * plan.held + which
        count = group_cells(plan, group_ref, class_ref, crop)
        mean, total = 0.0, 0.0
        for other, ref, block, held in entries:
            side = side_of(class_ref, other)
            weight = jnp.where(group_ref[other] == group_ref[crop], side * side, 0).astype(f32)
            mean = mean + weight * ref[2 * block, held]
        mean = mean / count
        for other, ref, block, held in entries:
            side = side_of(class_ref, other)
            same = group_ref[other] == group_ref[crop]
            spread = ref[2 * block, held] - mean
            total = total + jnp.where(same, 1.0, 0.0).astype(f32) * ref[2 * block + 1, held]
            total = total + jnp.where(same, side * side, 0).astype(f32) * (spread * spread)
        scale = lax.rsqrt(total / count + norm_eps)
        scales[which] = scale
        inside = crop_inside(plan, class_ref, dp_at, which, maps.shape[1:])
        values = (maps[which] * inside - mean[:, :1]) * inside * scale[:, :1]
        norm[which] = values
        pack_strips(plan, values, which, send)


def top_kernel(plan, class_ref, top, send):
    dp_at, _ = device_at()
    for which in range(plan.held):
        inside = crop_inside(plan, class_ref, dp_at, which, top.shape[1:])
        pack_strips(plan, top[which] * inside, which, send)


def first_kernel(plan, masks, class_ref, recv, *refs):
    n = plan.parts
    packets, refs = refs[:n], refs[n:]
    entry_norm, gains, first_out, alone, with_a, with_b, weight, even, odd = refs
    dp_at, chan_at = device_at()
    crop, strip = crop_strip(plan, dp_at, chan_at)
    rows = TAPS * plan.part + plan.part
    table = packets[0][0, rows : rows + 16]
    for j in range(1, plan.n_chan):
        table = table + packets[0][j, rows : rows + 16]
    gains[...] = table
    fill_weight(plan, masks, packets, weight)
    norm = recv[...].T
    entry_norm[...] = norm
    inside = inside_mask(plan, class_ref, crop, strip, plan.n_in, True)
    pre = norm * table[0:1] + table[1:2]
    fill_taps(plan, silu(pre) * inside, even, odd)
    out = conv_forward(plan, even, odd, weight)
    first_out[...] = out
    inside = inside_mask(plan, class_ref, crop, strip, plan.n_out, False)
    write_messages(strip, local_stats(plan, class_ref, crop, strip, out, inside), out, (alone, with_a, with_b))


def wide_rows(gains):
    return [jnp.concatenate([gains[4 + 2 * k : 5 + 2 * k], gains[5 + 2 * k : 6 + 2 * k]], axis=1) for k in range(5)]


def hidden_kernel(plan, masks, crop_masks, group_ref, class_ref, gains, first_out, edge_a, edge_b, entry_norm, *refs):
    n, m = plan.parts, plan.parts * 2
    narrow_packets, packets = refs[:n], refs[n:m]
    refs = refs[m:]
    tiles, refs = refs[:-10], refs[-10:]
    middle_norm, norm_rows, hidden, alone, with_a, with_b, weight, flat, even, odd = refs
    dp_at, chan_at = device_at()
    crop, strip = crop_strip(plan, dp_at, chan_at)
    wide = wide_rows(gains)
    mean, scale = group_stats(plan, group_ref, class_ref, crop, crop_entries(plan, tiles, crop_masks))
    norm_rows[...] = tile([mean, scale], plan.n_out)
    inside = inside_mask(plan, class_ref, crop, strip, plan.n_out, True)
    norm = (with_edges(plan, strip, first_out[...], edge_a, edge_b) - mean) * inside * scale
    middle_norm[...] = norm
    fill_taps(plan, silu(norm * wide[0] + wide[1]) * inside, even, odd)
    fill_weight(plan, masks, packets, weight)
    fill_flat(plan, masks, narrow_packets, TAPS * plan.part, flat)
    inside = inside[SIDE : SIDE + plan.cells]
    shortcut_in = (entry_norm[SIDE : SIDE + plan.cells] * gains[2:3] + gains[3:4]) * inside[:, : plan.n_in]
    out = conv_forward(plan, even, odd, weight) + dot3(split(shortcut_in), split(flat[...]), NT)
    out = out * inside
    hidden[...] = out
    write_messages(strip, local_stats(plan, class_ref, crop, strip, out, inside), out, (alone, with_a, with_b))


def top_back_kernel(plan, masks, recv, *refs):
    packets, (top_halo, out, weight, even, odd) = refs[: plan.parts], refs[plan.parts :]
    top = recv[...].T
    top_halo[...] = top
    fill_taps(plan, top, even, odd)
    fill_weight(plan, masks, packets, weight)
    out[...] = conv_backward(plan, even, odd, weight)


def decoder_kernel(plan, masks, crop_masks, group_ref, class_ref, gains, hidden, edge_a, edge_b, top_back, *refs):
    packets, refs = refs[: plan.parts], refs[plan.parts :]
    tiles, refs = refs[:-7], refs[-7:]
    decoder_norm, norm_rows, pre_grad, alone, with_a, with_b, style = refs
    dp_at, chan_at = device_at()
    crop, strip = crop_strip(plan, dp_at, chan_at)
    wide = wide_rows(gains)
    entries = crop_entries(plan, tiles, crop_masks)
    mean, scale = group_stats(plan, group_ref, class_ref, crop, entries)
    fill_flat(plan, masks, packets, TAPS * plan.part, style)
    pooled = entries[0][1][0:1]
    style_scale = lax.rsqrt(jnp.sum(pooled * pooled, axis=1, keepdims=True) + style_eps)
    style_vec = pooled * style_scale
    eight = jnp.broadcast_to(style_vec, (8, plan.n_out))
    term = lax.dot_general(eight, style[...], NT, precision=highest, preferred_element_type=f32)[0:1]
    shift = wide[3] + (term + wide[4])
    norm_rows[...] = tile(
        [mean, scale, shift, style_vec, jnp.broadcast_to(style_scale, (1, plan.n_out))], plan.n_out
    )
    inside = inside_mask(plan, class_ref, crop, strip, plan.n_out, True)
    norm = (with_edges(plan, strip, hidden[...], edge_a, edge_b) - mean) * inside * scale
    decoder_norm[...] = norm
    own = norm[SIDE : SIDE + plan.cells]
    grad = top_back[...] * silu_slope(own * wide[2] + shift) * inside[SIDE : SIDE + plan.cells]
    pre_grad[...] = grad
    write_messages(strip, tile([row_sum(grad), row_sum(grad * own)], plan.n_out), grad, (alone, with_a, with_b))


def out_kernel(plan, masks, class_ref, gains, hidden, decoder_norm, norm_rows, *refs):
    packets, (send, weight, even, odd) = refs[: plan.parts], refs[plan.parts :]
    dp_at, chan_at = device_at()
    crop, strip = crop_strip(plan, dp_at, chan_at)
    wide = wide_rows(gains)
    inside = inside_mask(plan, class_ref, crop, strip, plan.n_out, True)
    fill_taps(plan, silu(decoder_norm[...] * wide[2] + norm_rows[2:3]) * inside, even, odd)
    fill_weight(plan, masks, packets, weight)
    out = hidden[...] + conv_forward(plan, even, odd, weight) * inside[SIDE : SIDE + plan.cells]
    out = out.T
    for chan in range(plan.n_chan):
        send[chan] = out[chan * plan.out_own : (chan + 1) * plan.out_own]


def hidden_back_kernel(
    plan, masks, crop_masks, group_ref, class_ref, gains, pre_grad, edge_a, edge_b,
    decoder_norm, norm_rows, top_halo, middle_norm, *refs
):
    n, m = plan.parts, plan.parts * 2
    packets, style_packets = refs[:n], refs[n:m]
    refs = refs[m:]
    tiles, refs = refs[:-9], refs[-9:]
    hidden_grad, out, alone, with_a, with_b, weight, style, even, odd = refs
    dp_at, chan_at = device_at()
    crop, strip = crop_strip(plan, dp_at, chan_at)
    wide = wide_rows(gains)
    entries = crop_entries(plan, tiles, crop_masks)
    sums = group_sums(plan, group_ref, crop, entries, 2)
    count = group_cells(plan, group_ref, class_ref, crop)
    fill_flat(plan, masks, style_packets, TAPS * plan.part, style)
    style_vec, style_scale = norm_rows[3:4], norm_rows[4:5]
    eight = jnp.broadcast_to(entries[0][1][0:1], (8, plan.n_out))
    vec_grad = lax.dot_general(eight, style[...], NN, precision=highest, preferred_element_type=f32)[0:1]
    pooled_grad = style_scale * (vec_grad - style_vec * jnp.sum(vec_grad * style_vec, axis=1, keepdims=True))
    side = side_of(class_ref, crop)
    pooled_grad = pooled_grad / (side * side).astype(f32)
    grad = with_edges(plan, strip, pre_grad[...], edge_a, edge_b)
    inside = inside_mask(plan, class_ref, crop, strip, plan.n_out, True)
    grad = norm_rows[1:2] * wide[2] * (grad - sums[0:1] / count - decoder_norm[...] * (sums[1:2] / count))
    grad = top_halo[...] + (grad + pooled_grad) * inside
    hidden_grad[...] = grad
    fill_taps(plan, grad, even, odd)
    fill_weight(plan, masks, packets, weight)
    own = middle_norm[SIDE : SIDE + plan.cells]
    result = conv_backward(plan, even, odd, weight) * silu_slope(own * wide[0] + wide[1])
    result = result * inside[SIDE : SIDE + plan.cells]
    out[...] = result
    write_messages(strip, tile([row_sum(result), row_sum(result * own)], plan.n_out), result, (alone, with_a, with_b))


def first_back_kernel(
    plan, masks, crop_masks, group_ref, class_ref, gains, pre_grad, edge_a, edge_b,
    middle_norm, norm_rows, entry_norm, shortcut_grad, *refs
):
    packets, refs = refs[: plan.parts], refs[plan.parts :]
    tiles, refs = refs[:-6], refs[-6:]
    first_grad, sums_out, send, weight, even, odd = refs
    dp_at, chan_at = device_at()
    crop, strip = crop_strip(plan, dp_at, chan_at)
    wide = wide_rows(gains)
    sums = group_sums(plan, group_ref, crop, crop_entries(plan, tiles, crop_masks), 2)
    count = group_cells(plan, group_ref, class_ref, crop)
    grad = with_edges(plan, strip, pre_grad[...], edge_a, edge_b)
    inside = inside_mask(plan, class_ref, crop, strip, plan.n_out, True)
    grad = norm_rows[1:2] * wide[0] * (grad - sums[0:1] / count - middle_norm[...] * (sums[1:2] / count)) * inside
    first_grad[...] = grad[SIDE : SIDE + plan.cells]
    fill_taps(plan, grad, even, odd)
    fill_weight(plan, masks, packets, weight)
    own = entry_norm[SIDE : SIDE + plan.cells]
    result = conv_backward(plan, even, odd, weight) * silu_slope(own * gains[0:1] + gains[1:2])
    result = result * inside[SIDE : SIDE + plan.cells, : plan.n_in]
    other = shortcut_grad[...]
    sums_out[...] = tile(
        [row_sum(result), row_sum(result * own), row_sum(other), row_sum(other * own)], plan.n_in
    )
    joined = (result * gains[0:1] + other * gains[2:3]).T
    for chan in range(plan.n_chan):
        send[chan] = joined[chan * plan.in_own : (chan + 1) * plan.in_own]


def put_weight_rows(plan, value, t, keep, away):
    dp_at, chan_at = device_at()
    core = dp_at & 1
    for j in range(plan.n_chan):
        for q, ref in enumerate((keep, away)[: plan.parts]):
            ref[j, t * plan.part : (t + 1) * plan.part, :] = value[j, q]


def weight_grad(plan, grad, even, odd, keep, away, result):
    dp_at, chan_at = device_at()
    core = dp_at & 1
    left = split(grad.T)
    for a in range(3):
        for b in range(3):
            t = 3 * a + b
            result[...] = dot3(left, read_tap(plan, even, odd, a, b), NN)
            place_rows(plan, result, lambda ref, j: ref.at[j, t * plan.part : (t + 1) * plan.part], keep, away)


def place_rows(plan, result, target, keep, away):
    dp_at, chan_at = device_at()
    core = dp_at & 1
    for j in range(plan.n_chan):
        base = (chan_at ^ j) * plan.out_own
        if plan.parts == 1:
            target(keep, j)[...] = result[pl.ds(pl.multiple_of(base, 8), plan.part)]
            continue
        target(keep, j)[...] = result[pl.ds(pl.multiple_of(base + core * plan.part, 8), plan.part)]
        target(away, j)[...] = result[pl.ds(pl.multiple_of(base + (1 - core) * plan.part, 8), plan.part)]


def decoder_weight_kernel(plan, class_ref, gains, top_halo, decoder_norm, norm_rows, *refs):
    out, (result, even, odd) = refs[: plan.parts], refs[plan.parts :]
    dp_at, chan_at = device_at()
    crop, strip = crop_strip(plan, dp_at, chan_at)
    wide = wide_rows(gains)
    inside = inside_mask(plan, class_ref, crop, strip, plan.n_out, True)
    fill_taps(plan, silu(decoder_norm[...] * wide[2] + norm_rows[2:3]) * inside, even, odd)
    weight_grad(plan, top_halo[SIDE : SIDE + plan.cells], even, odd, out[0], out[-1], result)


def middle_weight_kernel(plan, class_ref, gains, hidden_grad, middle_norm, *refs):
    out, (result, even, odd) = refs[: plan.parts], refs[plan.parts :]
    dp_at, chan_at = device_at()
    crop, strip = crop_strip(plan, dp_at, chan_at)
    wide = wide_rows(gains)
    inside = inside_mask(plan, class_ref, crop, strip, plan.n_out, True)
    fill_taps(plan, silu(middle_norm[...] * wide[0] + wide[1]) * inside, even, odd)
    weight_grad(plan, hidden_grad[SIDE : SIDE + plan.cells], even, odd, out[0], out[-1], result)


def shortcut_kernel(plan, masks, class_ref, gains, hidden_grad, entry_norm, *refs):
    packets, refs = refs[: plan.parts], refs[plan.parts :]
    pre_grad, refs = refs[0], refs[1:]
    out, (result, flat) = refs[: plan.parts], refs[plan.parts :]
    dp_at, chan_at = device_at()
    crop, strip = crop_strip(plan, dp_at, chan_at)
    inside = inside_mask(plan, class_ref, crop, strip, plan.n_in, False)
    shortcut_in = (entry_norm[SIDE : SIDE + plan.cells] * gains[2:3] + gains[3:4]) * inside
    grad = hidden_grad[SIDE : SIDE + plan.cells]
    fill_flat(plan, masks, packets, TAPS * plan.part, flat)
    pre_grad[...] = dot3(split(grad), split(flat[...]), NN) * inside
    result[...] = dot3(split(grad.T), split(shortcut_in), NN)
    place_rows(plan, result, lambda ref, j: ref.at[j], out[0], out[-1])


def entry_weight_kernel(plan, class_ref, gains, first_grad, entry_norm, *refs):
    out, (result, even, odd) = refs[: plan.parts], refs[plan.parts :]
    dp_at, chan_at = device_at()
    crop, strip = crop_strip(plan, dp_at, chan_at)
    inside = inside_mask(plan, class_ref, crop, strip, plan.n_in, True)
    fill_taps(plan, silu(entry_norm[...] * gains[0:1] + gains[1:2]) * inside, even, odd)
    weight_grad(plan, first_grad[...], even, odd, out[0], out[-1], result)


def input_grad_kernel(plan, crop_masks, group_ref, class_ref, gains, recv, norm, scales, *refs):
    tiles, out = refs[:-1], refs[-1]
    dp_at, chan_at = device_at()
    entries = crop_entries(plan, tiles, crop_masks)
    for which in range(plan.held):
        crop = dp_at * plan.held + which
        count = group_cells(plan, group_ref, class_ref, crop)
        sums = group_sums(plan, group_ref, crop, entries, 4) / count
        shift = sums[0:1] * gains[0:1] + sums[2:3] * gains[2:3]
        slope = sums[1:2] * gains[0:1] + sums[3:4] * gains[2:3]
        first = pl.ds(pl.multiple_of(chan_at * plan.in_own, plan.in_own), plan.in_own)
        turned = jnp.concatenate([shift, slope, jnp.zeros((126, plan.n_in), f32)], axis=0).T
        lanes = lax.broadcasted_iota(jnp.int32, (plan.in_own, plan.n_in), 1)
        picked = lax.broadcasted_iota(jnp.int32, (plan.in_own, plan.n_in), 0) + chan_at * plan.in_own
        pick = jnp.where(lanes == picked, 1.0, 0.0).astype(f32)
        shift = jnp.sum(pick * shift, axis=1, keepdims=True)
        slope = jnp.sum(pick * slope, axis=1, keepdims=True)
        pieces = [recv[which * plan.strips + gray(strip)] for strip in range(plan.strips)]
        joined = jnp.concatenate(pieces, axis=1)[:, : SIDE * SIDE]
        inside = crop_inside(plan, class_ref, dp_at, which, joined.shape)
        out[which] = scales[which][:, :1] * (joined - shift - norm[which] * slope) * inside


def join_kernel(plan, recv, out):
    for which in range(plan.held):
        pieces = [recv[which * plan.strips + gray(strip)] for strip in range(plan.strips)]
        out[which] = jnp.concatenate(pieces, axis=1)[:, : SIDE * SIDE]


def run(kernel, smem, arrays, out_shapes, scratch=(), flops=0):
    shapes = [jax.ShapeDtypeStruct(shape, f32) for shape in out_shapes]
    moved = 4 * sum(int(a.size) for a in arrays) + 4 * sum(int(s.size) for s in shapes)
    return pl.pallas_call(
        kernel,
        out_shape=shapes,
        in_specs=[SMEM] * len(smem) + [VMEM] * len(arrays),
        out_specs=[VMEM] * len(shapes),
        scratch_shapes=list(scratch),
        cost_estimate=pl.CostEstimate(flops=flops, bytes_accessed=moved, transcendentals=0),
        compiler_params=pltpu.CompilerParams(vmem_limit_bytes=48 * 2**20),
    )(*smem, *arrays)


def adamw(weight, gradient, moment, square, rate, decay):
    first_new = beta_one * moment + (1.0 - beta_one) * gradient
    second_new = beta_two * square + (1.0 - beta_two) * gradient * gradient
    corrected_first = first_new / (1.0 - beta_one**STEP)
    corrected_second = second_new / (1.0 - beta_two**STEP)
    updated = weight - rate * (
        corrected_first / (jnp.sqrt(corrected_second) + adam_eps) + decay * weight
    )
    return (updated, first_new, second_new)


def make_body(mesh):
    def body(
        crop_maps, out_cotangent, norm_group, scale_class,
        entry_conv, middle_conv, shortcut_map, decoder_conv, style_map, narrow_gain_table, wide_gain_table,
        entry_moment, middle_moment, shortcut_moment, decoder_moment, style_moment, narrow_moment, wide_moment,
        entry_square, middle_square, shortcut_square, decoder_square, style_square, narrow_square, wide_square,
    ):
        plan = Plan(mesh, crop_maps.shape, out_cotangent.shape)
        n_in, n_out, n_chan = plan.n_in, plan.n_out, plan.n_chan
        cells, cells_halo, part = plan.cells, plan.cells_halo, plan.part
        dp_at, chan_at = lax.axis_index("dp"), lax.axis_index("chan")
        core = dp_at & 1
        ids = (norm_group, scale_class)

        def own_part(weight):
            if plan.parts == 1:
                return weight
            return lax.dynamic_slice_in_dim(weight, core * part, part, 0)

        def tap_rows(weight):
            return jnp.transpose(own_part(weight), (1, 0, 2)).reshape(TAPS * part, weight.shape[2])

        chan_stages = pair_bits(plan.chan_bits[::-1])

        def gather_packet(packet):
            gathered, masks = packet[None], [0]
            for stage in chan_stages:
                arrived = [swap(gathered, mask, plan) for mask in stage]
                gathered = jnp.concatenate([gathered] + arrived, axis=0)
                masks = masks + [held ^ mask for mask in stage for held in masks]
            if plan.parts == 1:
                return [gathered], masks
            return [gathered, swap(gathered, plan.core_mask, plan)], masks

        narrow_tile = lax.dynamic_update_slice(
            jnp.zeros((4, n_in), f32), narrow_gain_table, (jnp.int32(0), chan_at * plan.in_own)
        )
        wide_tile = lax.dynamic_update_slice(
            jnp.zeros((5, n_out), f32), wide_gain_table, (jnp.int32(0), chan_at * plan.out_own)
        )
        gain_rows = jnp.concatenate(
            [narrow_tile, wide_tile.reshape(10, n_in), jnp.zeros((2, n_in), f32)], axis=0
        )
        packet_a, masks = gather_packet(
            jnp.concatenate([tap_rows(entry_conv), own_part(shortcut_map), gain_rows], axis=0)
        )
        packet_b, _ = gather_packet(tap_rows(middle_conv))
        packet_c, _ = gather_packet(jnp.concatenate([tap_rows(decoder_conv), own_part(style_map)], axis=0))

        def dp_swap(block, mask):
            return lax.ppermute(block, "dp", [(i, i ^ mask) for i in range(plan.n_dp)])

        def gather_strips(messages, values):
            alone, with_a, with_b = messages
            if plan.quick:
                a, b = swap(with_a, plan.strip_bits[0], plan), swap(with_b, plan.strip_bits[1], plan)
                far = swap(alone, plan.strip_bits[0] ^ plan.strip_bits[1], plan)
                return [alone, a[:8], b[:8], far], [0, 1, 2, 3], a, b
            tiles, strip_masks = [alone], [0]
            for bit in plan.strip_bits:
                stacked = jnp.concatenate(tiles, axis=0)
                stacked = swap(stacked, bit, plan)
                tiles = tiles + [stacked[8 * k : 8 * k + 8] for k in range(len(tiles))]
                strip_masks = strip_masks + [mask ^ bit for mask in strip_masks]
            up, down = [], []
            for device in range(plan.n_all):
                low = (device % n_chan) % plan.strips
                strip, base = plan.strip_of[low], device - low
                if strip + 1 < plan.strips:
                    down.append((device, base + gray(strip + 1)))
                if strip > 0:
                    up.append((device, base + gray(strip - 1)))
            blank = jnp.zeros((8, values.shape[1]), f32)
            above = lax.ppermute(values[-SIDE:], BOTH, down)
            below = lax.ppermute(values[:SIDE], BOTH, up)
            return tiles, strip_masks, jnp.concatenate([blank, above]), jnp.concatenate([blank, below])

        def gather_crops(block):
            gathered, crop_masks = [block], [0]
            stages = [[plan.core_mask]] + pair_bits(plan.crop_bits + plan.far_bits)
            for stage in stages:
                joined = gathered[0] if len(gathered) == 1 else jnp.concatenate(gathered, axis=0)
                gathered = [joined] + [swap(joined, mask, plan) for mask in stage]
                crop_masks = crop_masks + [held ^ mask for mask in stage for held in crop_masks]
            return gathered, crop_masks

        own_crop = dp_at * plan.held + chan_at // plan.strips
        own_side = jnp.where(scale_class[own_crop] == 0, SIDE, H_SMALL)

        def strip_cells(mask):
            strip = jnp.array(plan.strip_of, jnp.int32)[(chan_at ^ mask) % plan.strips]
            return (jnp.clip(own_side - strip * plan.rows, 0, plan.rows) * own_side).astype(f32)

        def merge_stats(tiles, strip_masks):
            counts = [strip_cells(mask) for mask in strip_masks]
            mean = sum(n * t[0:1] for n, t in zip(counts, tiles)) / (own_side * own_side).astype(f32)
            squares = sum(t[1:2] + n * (t[0:1] - mean) * (t[0:1] - mean) for n, t in zip(counts, tiles))
            return jnp.concatenate([mean, squares, jnp.zeros((6, mean.shape[1]), f32)], axis=0)

        def merge_sums(tiles):
            return sum(tiles)

        message_shapes = [(8, n_out), (8 + SIDE, n_out), (8 + SIDE, n_out)]
        wide_weight, wide_taps = pltpu.VMEM((TAPS, n_out, n_out), f32), tap_scratch(plan, n_out)
        narrow_weight, narrow_taps = pltpu.VMEM((TAPS, n_out, n_in), f32), tap_scratch(plan, n_in)
        flat_narrow = pltpu.VMEM((n_out, n_in), f32)
        flat_wide = pltpu.VMEM((n_out, n_out), f32)
        wide_flops = 2 * 3 * TAPS * cells * n_out * n_out
        narrow_flops = 2 * 3 * TAPS * cells * n_out * n_in

        maps_shape = crop_maps.shape
        stats = run(
            functools.partial(stats_kernel, plan), (scale_class,), (crop_maps,),
            [(2, plan.held, plan.in_own, 128)],
        )[0]
        dp_tiles, dp_masks = [stats], [0]
        for stage in pair_bits(plan.dp_bits):
            joined = dp_tiles[0] if len(dp_tiles) == 1 else jnp.concatenate(dp_tiles, axis=0)
            dp_tiles = [joined] + [dp_swap(joined, mask) for mask in stage]
            dp_masks = dp_masks + [held ^ mask for mask in stage for held in dp_masks]
        norm_held, scales, send = run(
            functools.partial(norm_kernel, plan, dp_masks), ids, (crop_maps, *dp_tiles),
            [maps_shape, (plan.held, plan.in_own, 128), (n_chan, plan.in_own, cells_halo)],
        )
        recv = lax.all_to_all(send, "chan", 0, 0).reshape(n_in, cells_halo)

        entry_norm, gains, first_out, *messages = run(
            functools.partial(first_kernel, plan, masks), (scale_class,), (recv, *packet_a),
            [(cells_halo, n_in), (16, n_in), (cells, n_out)] + message_shapes,
            [narrow_weight] + narrow_taps, narrow_flops,
        )
        tiles, strip_masks, edge_a, edge_b = gather_strips(messages, first_out)
        crop_tiles, crop_masks = gather_crops(merge_stats(tiles, strip_masks))

        middle_norm, middle_rows, hidden, *messages = run(
            functools.partial(hidden_kernel, plan, masks, crop_masks), ids,
            (gains, first_out, edge_a, edge_b, entry_norm, *packet_a, *packet_b, *crop_tiles),
            [(cells_halo, n_out), (8, n_out), (cells, n_out)] + message_shapes,
            [wide_weight, flat_narrow] + wide_taps, wide_flops,
        )
        tiles, strip_masks, edge_a, edge_b = gather_strips(messages, hidden)
        pooled_tiles, _ = gather_crops(merge_stats(tiles, strip_masks))

        top_send = run(
            functools.partial(top_kernel, plan), (scale_class,), (out_cotangent,),
            [(n_chan, plan.out_own, cells_halo)],
        )[0]
        top_recv = lax.all_to_all(top_send, "chan", 0, 0).reshape(n_out, cells_halo)
        top_halo, top_back = run(
            functools.partial(top_back_kernel, plan, masks), (), (top_recv, *packet_c),
            [(cells_halo, n_out), (cells, n_out)], [wide_weight] + wide_taps, wide_flops,
        )

        decoder_norm, decoder_rows, decoder_pre_grad, *messages = run(
            functools.partial(decoder_kernel, plan, masks, crop_masks), ids,
            (gains, hidden, edge_a, edge_b, top_back, *packet_c, *pooled_tiles),
            [(cells_halo, n_out), (8, n_out), (cells, n_out)] + message_shapes,
            [flat_wide],
        )
        tiles, strip_masks, edge_a, edge_b = gather_strips(messages, decoder_pre_grad)
        decoder_tiles, _ = gather_crops(merge_sums(tiles))

        out_send = run(
            functools.partial(out_kernel, plan, masks), (scale_class,),
            (gains, hidden, decoder_norm, decoder_rows, *packet_c),
            [(n_chan, plan.out_own, cells)], [wide_weight] + wide_taps, wide_flops,
        )[0]
        out_recv = lax.all_to_all(out_send, "chan", 0, 0)
        block_out = run(functools.partial(join_kernel, plan), (), (out_recv,), [out_cotangent.shape])[0]
        wide_packet, narrow_packet = (n_chan, TAPS * part, n_out), (n_chan, TAPS * part, n_in)
        decoder_wgrad = run(
            functools.partial(decoder_weight_kernel, plan), (scale_class,),
            (gains, top_halo, decoder_norm, decoder_rows), [wide_packet] * plan.parts, [flat_wide] + wide_taps, wide_flops,
        )

        hidden_grad, middle_pre_grad, *messages = run(
            functools.partial(hidden_back_kernel, plan, masks, crop_masks), ids,
            (gains, decoder_pre_grad, edge_a, edge_b, decoder_norm, decoder_rows, top_halo, middle_norm,
             *packet_b, *packet_c, *decoder_tiles),
            [(cells_halo, n_out), (cells, n_out)] + message_shapes,
            [wide_weight, flat_wide] + wide_taps, wide_flops,
        )
        tiles, strip_masks, edge_a, edge_b = gather_strips(messages, middle_pre_grad)
        middle_tiles, _ = gather_crops(merge_sums(tiles))
        shortcut_grad, *shortcut_wgrad = run(
            functools.partial(shortcut_kernel, plan, masks), (scale_class,), (gains, hidden_grad, entry_norm, *packet_a),
            [(cells, n_in)] + [(n_chan, part, n_in)] * plan.parts, [flat_narrow, flat_narrow],
            2 * wide_flops // (TAPS * 2),
        )
        middle_wgrad = run(
            functools.partial(middle_weight_kernel, plan), (scale_class,), (gains, hidden_grad, middle_norm),
            [wide_packet] * plan.parts, [flat_wide] + wide_taps, wide_flops,
        )

        first_grad, entry_sums, send = run(
            functools.partial(first_back_kernel, plan, masks, crop_masks), ids,
            (gains, middle_pre_grad, edge_a, edge_b, middle_norm, middle_rows, entry_norm, shortcut_grad,
             *packet_a, *middle_tiles),
            [(cells, n_out), (8, n_in), (n_chan, plan.in_own, cells)],
            [narrow_weight] + wide_taps, narrow_flops,
        )
        entry_wgrad = run(
            functools.partial(entry_weight_kernel, plan), (scale_class,), (gains, first_grad, entry_norm),
            [narrow_packet] * plan.parts, [flat_narrow] + narrow_taps, narrow_flops,
        )
        recv = lax.all_to_all(send, "chan", 0, 0)
        entry_block, entry_masks = [entry_sums], [0]
        strip_total = entry_sums
        for stage in pair_bits(plan.strip_bits):
            strip_total = strip_total + sum(swap(strip_total, mask, plan) for mask in stage)
        entry_tiles, _ = gather_crops(strip_total)
        input_grad = run(
            functools.partial(input_grad_kernel, plan, crop_masks), ids,
            (gains, recv, norm_held, scales, *entry_tiles), [maps_shape],
        )[0]

        def reduce_packet(grads):
            total = grads[0]
            if plan.parts == 2:
                total = total + swap(grads[1], plan.core_mask, plan)
            blocks = [total[j] for j in range(n_chan)]
            for bit in plan.chan_bits[:1]:
                sent = jnp.stack([blocks[j] for j in range(n_chan) if j & bit])
                arrived = swap(sent, bit, plan)
                blocks = [blocks[2 * k] + arrived[k] for k in range(n_chan // 2)]
            total = blocks[0]
            for k in range(1, len(blocks)):
                total = total + swap(blocks[k], 2 * k, plan)
            for bit in plan.far_bits + ([plan.core_mask] if plan.parts == 1 else []):
                total = total + swap(total, bit, plan)
            if plan.parts == 1:
                return [total]
            other = swap(total, plan.core_mask, plan)
            return [jnp.where(core == 0, total, other), jnp.where(core == 0, other, total)]

        def from_taps(pieces):
            width = pieces[0].shape[-1]
            return jnp.concatenate(
                [jnp.transpose(p.reshape(TAPS, part, width), (1, 0, 2)) for p in pieces], axis=0
            )

        decoder_sum = from_taps(reduce_packet(decoder_wgrad))
        middle_sum = from_taps(reduce_packet(middle_wgrad))
        shortcut_sum = jnp.concatenate(reduce_packet(shortcut_wgrad), axis=0)
        entry_sum = from_taps(reduce_packet(entry_wgrad))

        def stack_crops(tiles):
            return jnp.concatenate(tiles, axis=0).reshape(plan.n_crops, 8, -1)

        def own_columns(rows, size):
            return lax.dynamic_slice_in_dim(rows, chan_at * size, size, 1)

        pooled_all, decoder_all = stack_crops(pooled_tiles)[:, 0], stack_crops(decoder_tiles)
        style_vecs = pooled_all * lax.rsqrt(jnp.sum(pooled_all * pooled_all, axis=1, keepdims=True) + style_eps)
        style_sum = jnp.einsum(
            "no,nc->oc", own_columns(decoder_all[:, 0], plan.out_own), style_vecs, precision=highest
        )
        decoder_total = jnp.sum(decoder_all, axis=0)
        middle_total = jnp.sum(stack_crops(middle_tiles), axis=0)
        entry_total = jnp.sum(stack_crops(entry_tiles), axis=0)
        narrow_sum = own_columns(
            jnp.stack([entry_total[1], entry_total[0], entry_total[3], entry_total[2]]), plan.in_own
        )
        wide_sum = own_columns(
            jnp.stack([middle_total[1], middle_total[0], decoder_total[1], decoder_total[0], decoder_total[0]]),
            plan.out_own,
        )

        gradients = (entry_sum, middle_sum, shortcut_sum, decoder_sum, style_sum, narrow_sum, wide_sum)
        local_squares = jnp.zeros((), f32)
        for gradient in gradients:
            local_squares = local_squares + jnp.sum(gradient * gradient)
        total_squares = jnp.broadcast_to(local_squares, (8, 128))
        for stage in pair_bits(plan.chan_bits):
            total_squares = total_squares + sum(swap(total_squares, mask, plan) for mask in stage)
        grad_norm = jnp.sqrt(total_squares[0, 0])
        clip_factor = jnp.minimum(1.0, clip_bound / grad_norm)
        params = (entry_conv, middle_conv, shortcut_map, decoder_conv, style_map, narrow_gain_table, wide_gain_table)
        moments = (
            entry_moment, middle_moment, shortcut_moment, decoder_moment, style_moment, narrow_moment, wide_moment,
        )
        squares = (
            entry_square, middle_square, shortcut_square, decoder_square, style_square, narrow_square, wide_square,
        )
        rates = (0.06, 0.04, 0.16, 0.04, 1.0, 0.4, 0.4)
        decays = (decay_rate, decay_rate, decay_rate, decay_rate, decay_rate, 0.0, 0.0)
        results = [block_out, input_grad]
        for which in range(7):
            results.extend(
                adamw(
                    params[which], gradients[which] * clip_factor, moments[which], squares[which],
                    rates[which], decays[which],
                )
            )
        return tuple(results) + (grad_norm,)

    return body


def solution(mesh):
    maps, whole = P("dp", "chan", None), P()
    conv_spec, flat_spec, table_spec = P("chan", None, None), P("chan", None), P(None, "chan")
    params = (conv_spec, conv_spec, flat_spec, conv_spec, flat_spec, table_spec, table_spec)
    updated = tuple(spec for spec in params for _ in range(3))
    return jax.shard_map(
        make_body(mesh),
        mesh=mesh,
        in_specs=(maps, maps, whole, whole) + params * 3,
        out_specs=(maps, maps) + updated + (whole,),
        check_vma=False,
    )
```

time: 1140 us -> 363 us (0.32)
  waiting for transfers between devices: 514 us -> 111 us
  local copies, waits for them, and re-layouts: 285 us -> 32 us
  matrix products: 122 us -> 0.83 us
  blocking collectives: 121 us -> 0 us
  starting transfers between devices: 0.37 us -> 114 us
  Pallas kernels: 0 us -> 62.6 us
  other arithmetic: 65 us -> 25.2 us
    reduce_scatter x4 -> x0, waiting for transfers between devices: 324 us -> none  [the longest x2 170 us: conv_back(): lax.psum_scatter(partial_sum, 'chan', scatter_dimension=1, tiled=True)]
    all_gather x4 -> x0, waiting for transfers between devices: 178 us -> none  [the longest x1 74.4 us: body(): whole_decoder = lax.all_gather(decoder_in, 'chan', axis=1, tiled=True)]
    another operation x52 -> x2, local copies, waits for them, and re-layouts: 133 us -> 0.03 us  [the longest x1 0.03 us: body(): jnp.stack([middle_total[1], middle_total[0], decoder_total[1], decoder_to...]
    dot_general x42 -> x1, matrix products: 122 us -> 0.83 us  [body(): jnp.einsum('no,nc->oc', own_columns(decoder_all[:, 0], plan.out_own), sty...]
    ppermute x0 -> x85, waiting for transfers between devices: none -> 111 us  [the longest x82 111 us: swap(): return lax.ppermute(block, BOTH, [(i, i ^ mask) for i in range(plan.n_all)])]
    psum x11 -> x0, blocking collectives: 102 us -> none  [the longest x3 23 us: normalization_backward(): totals = lax.psum(jnp.stack(gradient_portions), 'dp')]
    ppermute x0 -> x85, starting transfers between devices: none -> 94.8 us  [the longest x82 91.8 us: swap(): return lax.ppermute(block, BOTH, [(i, i ^ mask) for i in range(plan.n_all)])]
    slice x14 -> x8, local copies, waits for them, and re-layouts: 72.2 us -> 0.64 us  [the longest x1 0.51 us: body(): grad_norm = jnp.sqrt(total_squares[0, 0])]
  transfers between devices with their start and end apart: 9 -> 89, of which waited for: 8 -> 32; matrix products, arithmetic and copies ran while one was open for 16% -> 11% of each run, Pallas kernels for 0% -> 15%
where the time goes in v1:
time: 363 us; the launch traced here: 358 us
  starting transfers between devices  114 us (31%)
  waiting for transfers between devices  111 us (31%)
  Pallas kernels  62.6 us (17%)
  local copies, waits for them, and re-layouts  32 us (9%)
  other arithmetic  25.2 us (7%)
  between operations  12.2 us (3%)
    ppermute x82, waiting for transfers between devices, swap(): return lax.ppermute(block, BOTH, [(i, i ^ mask) for i in range(plan.n_all)])  111 us
    ppermute x82, starting transfers between devices, swap(): return lax.ppermute(block, BOTH, [(i, i ^ mask) for i in range(plan.n_all)])  91.8 us
    pallas_call x16, Pallas kernels, run(): pl.pallas_call(kernel, out_shape=shapes, in_specs=[SMEM] * len(smem) + [V...  62.6 us
    unnamed x168, local copies, waits for them, and re-layouts  16.2 us
  transfers between devices with their start and end apart: 89, of which 32 were waited for; matrix products, arithmetic and copies ran while one was open for 11% of the time, Pallas kernels for 15%

profile of v1, /device:TPU:0, one launch (start us, length us, event | category | flops | bytes accessed | tf_op | source)
XLA Modules:
  0.0 358.2 jit_solution(8636934959398384158)
XLA Ops:
  9.6 4.1 %collective-permute-start.5 = (f32[1,176,128]{2,1,0:T(8,128)S(1)}, f32[1,176,128]{2,1,0:T(8,128)S(1)}, u32[]{:S(2)}, u32[]{:S(2)}) collective-permute-start(f32[1,176,128]{2,1,0:T(8,128)S(1)} %bitcast.127), channel_id=1, source_target_pairs={{0,6},{1,7},{2,4},{3,5},{4,2},{5,3},{6,0},{7,1},{8,14},{9,15},{10,... | collective-permute-start | bytes 270344 | tf_op jit(solution)/shard_map/ppermute | solution.py:70
  26.1 4.2 %all-to-all-start = ((f32[8,16,896]{2,1,0:T(8,128)}), f32[8,16,896]{2,1,0:T(8,128)}, u32[]{:S(2)}, u32[]{:S(2)}) async-start(f32[8,16,896]{2,1,0:T(8,128)} %get-tuple-element.64), calls=%async_computation | async-start | bytes 917504 | tf_op jit(solution)/shard_map/all_to_all | solution.py:765
  39.4 18.4 %collective-permute-done.10 = f32[1,144,256]{2,1,0:T(8,128)S(1)} collective-permute-done((f32[1,144,256]{2,1,0:T(8,128)S(1)}, f32[1,144,256]{2,1,0:T(8,128)S(1)}, u32[]{:S(2)}, u32[]{:S(2)}) %collective-permute-start.10) | collective-permute-done | bytes 147488 | tf_op jit(solution)/shard_map/ppermute | solution.py:70
  76.6 5.8 %all-to-all-start.1 = ((f32[8,32,896]{2,1,0:T(8,128)}), f32[8,32,896]{2,1,0:T(8,128)S(1)}, u32[]{:S(2)}, u32[]{:S(2)}) async-start(f32[8,32,896]{2,1,0:T(8,128)} %shard_map.500), calls=%async_computation.1 | async-start | bytes 1835008 | tf_op jit(solution)/shard_map/all_to_all | solution.py:788
  82.4 5.1 %shard_map.498 = (f32[896,128]{1,0:T(8,128)S(1)}, f32[16,128]{1,0:T(8,128)S(1)}, f32[784,256]{1,0:T(8,128)S(1)}, f32[8,256]{1,0:T(8,128)S(1)}, f32[64,256]{1,0:T(8,128)S(1)}, /*index=5*/f32[64,256]{1,0:T(8,128)S(1)}) custom-call(s32[8]{0:T(128)S(1)} %copy-done.22, f32[128,896]{1,0:T(8,128)} %bitcast.recv, ...), custom_call_target="tpu_custom_call" | custom-call | flops 1387266048 | bytes 3309568 | tf_op jit(solution)/shard_map/pallas_call | solution.py:619
  91.2 7.5 %collective-permute-done.15 = f32[8,256]{1,0:T(8,128)S(1)} collective-permute-done((f32[8,256]{1,0:T(8,128)S(1)}, f32[8,256]{1,0:T(8,128)S(1)}, u32[]{:S(2)}, u32[]{:S(2)}) %collective-permute-start.15) | collective-permute-done | bytes 8224 | tf_op jit(solution)/shard_map/ppermute | solution.py:70
  98.7 4.2 %collective-permute-done.8.edge_a = f32[64,256]{1,0:T(8,128)S(1)} collective-permute-done((f32[64,256]{1,0:T(8,128)S(1)}, f32[64,256]{1,0:T(8,128)S(1)}, u32[]{:S(2)}, u32[]{:S(2)}) %collective-permute-start.8) | collective-permute-done | bytes 65568 | tf_op jit(solution)/shard_map/ppermute | solution.py:70
  111.2 6.4 %shard_map.499 = (f32[896,256]{1,0:T(8,128)S(1)}, f32[8,256]{1,0:T(8,128)S(1)}, f32[784,256]{1,0:T(8,128)S(1)}, f32[8,256]{1,0:T(8,128)S(1)}, f32[64,256]{1,0:T(8,128)S(1)}, /*index=5*/f32[64,256]{1,0:T(8,128)S(1)}) custom-call(s32[8]{0:T(128)S(1)} %copy-done.25, s32[8]{0:T(128)S(1)} %copy-done.22, f32[16,128]{1,0:T(8,128)S(1)} %get-tuple-element.65.gains, ...), custom_call_target="tpu_custom_call" | custom-call | flops 2774532096 | bytes 7135232 | tf_op jit(solution)/shard_map/pallas_call | solution.py:619
  120.6 4.1 %collective-permute-start.21 = (f32[64,256]{1,0:T(8,128)S(1)}, f32[64,256]{1,0:T(8,128)S(1)}, u32[]{:S(2)}, u32[]{:S(2)}) collective-permute-start(f32[64,256]{1,0:T(8,128)S(1)} %get-tuple-element.73), channel_id=1, source_target_pairs={{0,2},{1,3},{2,0},{3,1},{4,6},{5,7},{6,4},{7,5},{8,10},{9,11},{10,... | collective-permute-start | bytes 196616 | tf_op jit(solution)/shard_map/ppermute | solution.py:70
  124.7 4.5 %collective-permute-done.27 = f32[8,256]{1,0:T(8,128)S(1)} collective-permute-done((f32[8,256]{1,0:T(8,128)S(1)}, f32[8,256]{1,0:T(8,128)S(1)}, u32[]{:S(2)}, u32[]{:S(2)}) %collective-permute-start.27) | collective-permute-done | bytes 8224 | tf_op jit(solution)/shard_map/ppermute | solution.py:70
  138.9 6.6 %concatenate.98 = f32[64,256]{1,0:T(8,128)} concatenate(f32[1,256]{1,0:T(1,128)} %copy-done.64, f32[1,256]{1,0:T(1,128)} %copy-done.63, f32[6,256]{1,0:T(8,128)} %copy-done.50, f32[8,256]{1,0:T(8,128)} %copy-done.57, f32[16,256]{1,0:T(8,128)} %collective-permute-done.29.refs_3_, f32[16,256]{1,0:T(8,128)} %collective-permute-done.30.refs_4_, f32[16,256]{1,0:T(8,128)} %collective-permute-done.31.refs_5_), dimensions={0} | concatenate | bytes 131072 | tf_op jit(solution)/shard_map/concatenate | solution.py:888
  158.0 6.2 %shard_map.511 = (f32[8,144,256]{2,1,0:T(8,128)S(1)}, f32[8,144,256]{2,1,0:T(8,128)}) custom-call(s32[8]{0:T(128)S(1)} %copy-done.22, f32[16,128]{1,0:T(8,128)S(1)} %get-tuple-element.65.gains, f32[896,256]{1,0:T(8,128)S(1)} %get-tuple-element.81.top_halo, f32[896,256]{1,0:T(8,128)S(1)} %get-tuple-element.76.decoder_norm, ...), custom_call_target="tpu_custom_call" | custom-call | flops 2774532096 | bytes 4210688 | tf_op jit(solution)/shard_map/pallas_call | solution.py:619
  164.9 5.2 %shard_map.503 = f32[8,32,784]{2,1,0:T(8,128)} custom-call(s32[8]{0:T(128)S(1)} %copy-done.22, f32[16,128]{1,0:T(8,128)S(1)} %get-tuple-element.65.gains, f32[784,256]{1,0:T(8,128)S(1)} %copy-done.12, f32[896,256]{1,0:T(8,128)S(1)} %get-tuple-element.76.decoder_norm, f32[8,256]{1,0:T(8,128)S(1)} %get-tuple-element.77.norm_rows, ...), custom_call_target="tpu_custom_call" | custom-call | flops 2774532096 | bytes 5160960 | tf_op jit(solution)/shard_map/pallas_call | solution.py:619
  174.5 4.6 %collective-permute-done.36.refs_5_ = f32[16,256]{1,0:T(8,128)S(1)} collective-permute-done((f32[16,256]{1,0:T(8,128)S(1)}, f32[16,256]{1,0:T(8,128)S(1)}, u32[]{:S(2)}, u32[]{:S(2)}) %collective-permute-start.36) | collective-permute-done | bytes 16416 | tf_op jit(solution)/shard_map/ppermute | solution.py:70
  179.2 6.8 %shard_map.505 = (f32[896,256]{1,0:T(8,128)S(1)}, f32[784,256]{1,0:T(8,128)S(1)}, f32[8,256]{1,0:T(8,128)S(1)}, f32[64,256]{1,0:T(8,128)S(1)}, f32[64,256]{1,0:T(8,128)S(1)}) custom-call(s32[8]{0:T(128)S(1)} %copy-done.25, s32[8]{0:T(128)S(1)} %copy-done.22, f32[16,128]{1,0:T(8,128)S(1)} %get-tuple-element.65.gains, ...), custom_call_target="tpu_custom_call" | custom-call | flops 2774532096 | bytes 10608640 | tf_op jit(solution)/shard_map/pallas_call | solution.py:619
  189.5 6.2 %shard_map.510 = (f32[8,144,256]{2,1,0:T(8,128)S(1)}, f32[8,144,256]{2,1,0:T(8,128)}) custom-call(s32[8]{0:T(128)S(1)} %copy-done.22, f32[16,128]{1,0:T(8,128)S(1)} %get-tuple-element.65.gains, f32[896,256]{1,0:T(8,128)S(1)} %get-tuple-element.88.hidden_grad, f32[896,256]{1,0:T(8,128)S(1)} %copy-done.27), custom_call_target="tpu_custom_call" | custom-call | flops 2774532096 | bytes 4202496 | tf_op jit(solution)/shard_map/pallas_call | solution.py:619
  208.9 5.6 %shard_map.507 = (f32[784,256]{1,0:T(8,128)S(1)}, f32[8,128]{1,0:T(8,128)S(1)}, f32[8,16,784]{2,1,0:T(8,128)}) custom-call(s32[8]{0:T(128)S(1)} %copy-done.25, s32[8]{0:T(128)S(1)} %copy-done.22, f32[16,128]{1,0:T(8,128)S(1)} %get-tuple-element.65.gains, f32[784,256]{1,0:T(8,128)S(1)} %get-tuple-element.84.pre_grad, ...), custom_call_target="tpu_custom_call" | custom-call | flops 1387266048 | bytes 5443584 | tf_op jit(solution)/shard_map/pallas_call | solution.py:619
  218.8 4.6 %all-to-all-start.3 = ((f32[8,16,784]{2,1,0:T(8,128)}), f32[8,16,784]{2,1,0:T(8,128)S(1)}, u32[]{:S(2)}, u32[]{:S(2)}) async-start(f32[8,16,784]{2,1,0:T(8,128)} %get-tuple-element.91), calls=%async_computation.3 | async-start | bytes 917504 | tf_op jit(solution)/shard_map/all_to_all | solution.py:846
  224.6 5.3 %shard_map.509 = (f32[8,144,128]{2,1,0:T(8,128)S(1)}, f32[8,144,128]{2,1,0:T(8,128)}) custom-call(s32[8]{0:T(128)S(1)} %copy-done.22, f32[16,128]{1,0:T(8,128)S(1)} %get-tuple-element.65.gains, f32[784,256]{1,0:T(8,128)S(1)} %copy-done.29, f32[896,128]{1,0:T(8,128)S(1)} %copy-done.14), custom_call_target="tpu_custom_call" | custom-call | flops 1387266048 | bytes 2449408 | tf_op jit(solution)/shard_map/pallas_call | solution.py:619
  271.4 7.4 %collective-permute-done.75 = f32[4,144,256]{2,1,0:T(8,128)S(1)} collective-permute-done((f32[4,144,256]{2,1,0:T(8,128)S(1)}, f32[4,144,256]{2,1,0:T(8,128)S(1)}, u32[]{:S(2)}, u32[]{:S(2)}) %collective-permute-start.75) | collective-permute-done | bytes 589856 | tf_op jit(solution)/shard_map/ppermute | solution.py:70
  287.9 4.5 %all-to-all-start.2 = ((f32[8,32,784]{2,1,0:T(8,128)}), f32[8,32,784]{2,1,0:T(8,128)S(1)}, u32[]{:S(2)}, u32[]{:S(2)}) async-start(f32[8,32,784]{2,1,0:T(8,128)} %shard_map.503), calls=%async_computation.2 | async-start | bytes 1835008 | tf_op jit(solution)/shard_map/all_to_all | solution.py:808
  300.0 9.6 %collective-permute-done.62 = f32[144,256]{1,0:T(8,128)S(1)} collective-permute-done((f32[144,256]{1,0:T(8,128)}, f32[144,256]{1,0:T(8,128)S(1)}, u32[]{:S(2)}, u32[]{:S(2)}) %collective-permute-start.62) | collective-permute-done | bytes 147488 | tf_op jit(solution)/shard_map/ppermute | solution.py:70
  310.2 4.6 %collective-permute-done.64 = f32[144,256]{1,0:T(8,128)S(1)} collective-permute-done((f32[144,256]{1,0:T(8,128)}, f32[144,256]{1,0:T(8,128)S(1)}, u32[]{:S(2)}, u32[]{:S(2)}) %collective-permute-start.64) | collective-permute-done | bytes 147488 | tf_op jit(solution)/shard_map/ppermute | solution.py:70
  314.8 10.6 %collective-permute-done.63 = f32[144,256]{1,0:T(8,128)S(1)} collective-permute-done((f32[144,256]{1,0:T(8,128)}, f32[144,256]{1,0:T(8,128)S(1)}, u32[]{:S(2)}, u32[]{:S(2)}) %collective-permute-start.63) | collective-permute-done | bytes 147488 | tf_op jit(solution)/shard_map/ppermute | solution.py:70
  (434 shorter events, 193.9 us)
Async XLA Ops:
  9.6 20.7 %collective-permute-start.5 = (f32[1,176,128]{2,1,0:T(8,128)S(1)}, f32[1,176,128]{2,1,0:T(8,128)S(1)}, u32[]{:S(2)}, u32[]{:S(2)}) collective-permute-start(f32[1,176,128]{2,1,0:T(8,128)S(1)} %bitcast.127), channel_id=1, source_target_pairs={{0,6},{1,7},{2,4},{3,5},{4,2},{5,3},{6,0},{7,1},{8,14},{9,15},{10,... | collective-permute-start | bytes 270344 | tf_op jit(solution)/shard_map/ppermute | solution.py:70
  13.7 19.6 %collective-permute-start.4 = (f32[1,176,128]{2,1,0:T(8,128)S(1)}, f32[1,176,128]{2,1,0:T(8,128)S(1)}, u32[]{:S(2)}, u32[]{:S(2)}) collective-permute-start(f32[1,176,128]{2,1,0:T(8,128)S(1)} %bitcast.128), channel_id=1, source_target_pairs={{0,2},{1,3},{2,0},{3,1},{4,6},{5,7},{6,4},{7,5},{8,10},{9,11},{10,... | collective-permute-start | bytes 270344 | tf_op jit(solution)/shard_map/ppermute | solution.py:70
  15.2 19.6 %collective-permute-start.3 = (f32[1,176,128]{2,1,0:T(8,128)S(1)}, f32[1,176,128]{2,1,0:T(8,128)S(1)}, u32[]{:S(2)}, u32[]{:S(2)}) collective-permute-start(f32[1,176,128]{2,1,0:T(8,128)S(1)} %bitcast.129), channel_id=1, source_target_pairs={{0,4},{1,5},{2,6},{3,7},{4,0},{5,1},{6,2},{7,3},{8,12},{9,13},{10,... | collective-permute-start | bytes 270344 | tf_op jit(solution)/shard_map/ppermute | solution.py:70
  26.1 50.5 %all-to-all-start = ((f32[8,16,896]{2,1,0:T(8,128)}), f32[8,16,896]{2,1,0:T(8,128)}, u32[]{:S(2)}, u32[]{:S(2)}) async-start(f32[8,16,896]{2,1,0:T(8,128)} %get-tuple-element.64), calls=%async_computation | async-start | bytes 917504 | tf_op jit(solution)/shard_map/all_to_all | solution.py:765
  30.3 27.5 %collective-permute-start.10 = (f32[1,144,256]{2,1,0:T(8,128)S(1)}, f32[1,144,256]{2,1,0:T(8,128)S(1)}, u32[]{:S(2)}, u32[]{:S(2)}) collective-permute-start(f32[1,144,256]{2,1,0:T(8,128)S(1)} %bitcast.115), channel_id=1, source_target_pairs={{0,4},{1,5},{2,6},{3,7},{4,0},{5,1},{6,2},{7,3},{8,12},{9,13},{10,... | collective-permute-start | bytes 442376 | tf_op jit(solution)/shard_map/ppermute | solution.py:70
  33.3 38.9 %collective-permute-start.24 = (f32[1,160,256]{2,1,0:T(8,128)}, f32[1,160,256]{2,1,0:T(8,128)S(1)}, u32[]{:S(2)}, u32[]{:S(2)}) collective-permute-start(f32[1,160,256]{2,1,0:T(8,128)} %maximum_bitcast_fusion), channel_id=1, source_target_pairs={{0,6},{1,7},{2,4},{3,5},{4,2},{5,3},{6,0},{7,1},{8,14},{9,15},{10,... | collective-permute-start | bytes 491528 | tf_op jit(solution)/shard_map/ppermute | solution.py:70
  34.8 26.2 %collective-permute-start.6 = (f32[4,176,128]{2,1,0:T(8,128)S(1)}, f32[4,176,128]{2,1,0:T(8,128)S(1)}, u32[]{:S(2)}, u32[]{:S(2)}) collective-permute-start(f32[4,176,128]{2,1,0:T(8,128)S(1)} %pad_maximum_fusion.4), channel_id=1, source_target_pairs={{0,1},{1,0},{2,3},{3,2},{4,5},{5,4},{6,7},{7,6},{8,9},{9,8},{10,11... | collective-permute-start | bytes 1081352 | tf_op jit(solution)/shard_map/ppermute | solution.py:70
  36.4 35.8 %collective-permute-start.23 = (f32[1,160,256]{2,1,0:T(8,128)}, f32[1,160,256]{2,1,0:T(8,128)S(1)}, u32[]{:S(2)}, u32[]{:S(2)}) collective-permute-start(f32[1,160,256]{2,1,0:T(8,128)} %maximum_bitcast_fusion), channel_id=1, source_target_pairs={{0,2},{1,3},{2,0},{3,1},{4,6},{5,7},{6,4},{7,5},{8,10},{9,11},{10,... | collective-permute-start | bytes 491528 | tf_op jit(solution)/shard_map/ppermute | solution.py:70
  36.5 35.7 %collective-permute-start.22 = (f32[1,160,256]{2,1,0:T(8,128)}, f32[1,160,256]{2,1,0:T(8,128)}, u32[]{:S(2)}, u32[]{:S(2)}) collective-permute-start(f32[1,160,256]{2,1,0:T(8,128)} %maximum_bitcast_fusion), channel_id=1, source_target_pairs={{0,4},{1,5},{2,6},{3,7},{4,0},{5,1},{6,2},{7,3},{8,12},{9,13},{10,... | collective-permute-start | bytes 491528 | tf_op jit(solution)/shard_map/ppermute | solution.py:70
  61.1 21.3 %collective-permute-start.7 = (f32[8,176,128]{2,1,0:T(8,128)S(1)}, f32[8,176,128]{2,1,0:T(8,128)}, u32[]{:S(2)}, u32[]{:S(2)}) collective-permute-start(f32[8,176,128]{2,1,0:T(8,128)S(1)} %constant_dynamic-update-slice_fusion.refs_0_), channel_id=1, source_target_pairs={{0,8},{1,9},{2,10},{3,11},{4,12},{5,13},{6,14},{7,15},{8,0},{9,1},... | collective-permute-start | bytes 2162696 | tf_op jit(solution)/shard_map/ppermute | solution.py:70
  72.2 39.0 %collective-permute-start.14 = (f32[8,144,256]{2,1,0:T(8,128)}, f32[8,144,256]{2,1,0:T(8,128)}, u32[]{:S(2)}, u32[]{:S(2)}) collective-permute-start(f32[8,144,256]{2,1,0:T(8,128)} %constant_dynamic-update-slice_fusion.5.refs_2_.refs_0_), channel_id=1, source_target_pairs={{0,8},{1,9},{2,10},{3,11},{4,12},{5,13},{6,14},{7,15},{8,0},{9,1},... | collective-permute-start | bytes 3538952 | tf_op jit(solution)/shard_map/ppermute | solution.py:70
  74.1 34.5 %collective-permute-start.25 = (f32[4,160,256]{2,1,0:T(8,128)}, f32[4,160,256]{2,1,0:T(8,128)}, u32[]{:S(2)}, u32[]{:S(2)}) collective-permute-start(f32[4,160,256]{2,1,0:T(8,128)} %pad_maximum_fusion), channel_id=1, source_target_pairs={{0,1},{1,0},{2,3},{3,2},{4,5},{5,4},{6,7},{7,6},{8,9},{9,8},{10,11... | collective-permute-start | bytes 1966088 | tf_op jit(solution)/shard_map/ppermute | solution.py:70
  76.6 71.4 %all-to-all-start.1 = ((f32[8,32,896]{2,1,0:T(8,128)}), f32[8,32,896]{2,1,0:T(8,128)S(1)}, u32[]{:S(2)}, u32[]{:S(2)}) async-start(f32[8,32,896]{2,1,0:T(8,128)} %shard_map.500), calls=%async_computation.1 | async-start | bytes 1835008 | tf_op jit(solution)/shard_map/all_to_all | solution.py:788
  109.8 38.2 %collective-permute-start.26 = (f32[8,160,256]{2,1,0:T(8,128)S(1)}, f32[8,160,256]{2,1,0:T(8,128)S(1)}, u32[]{:S(2)}, u32[]{:S(2)}) collective-permute-start(f32[8,160,256]{2,1,0:T(8,128)S(1)} %constant_dynamic-update-slice_fusion.10.refs_0_.refs_2_), channel_id=1, source_target_pairs={{0,8},{1,9},{2,10},{3,11},{4,12},{5,13},{6,14},{7,15},{8,0},{9,1},... | collective-permute-start | bytes 3932168 | tf_op jit(solution)/shard_map/ppermute | solution.py:70
  164.3 95.8 %collective-permute-start.74 = (f32[8,144,256]{2,1,0:T(8,128)}, f32[8,144,256]{2,1,0:T(8,128)}, u32[]{:S(2)}, u32[]{:S(2)}) collective-permute-start(f32[8,144,256]{2,1,0:T(8,128)} %get-tuple-element.103), channel_id=1, source_target_pairs={{0,8},{1,9},{2,10},{3,11},{4,12},{5,13},{6,14},{7,15},{8,0},{9,1},... | collective-permute-start | bytes 3538952 | tf_op jit(solution)/shard_map/ppermute | solution.py:70
  199.8 62.7 %collective-permute-start.60 = (f32[8,144,256]{2,1,0:T(8,128)}, f32[8,144,256]{2,1,0:T(8,128)}, u32[]{:S(2)}, u32[]{:S(2)}) collective-permute-start(f32[8,144,256]{2,1,0:T(8,128)} %get-tuple-element.99), channel_id=1, source_target_pairs={{0,8},{1,9},{2,10},{3,11},{4,12},{5,13},{6,14},{7,15},{8,0},{9,1},... | collective-permute-start | bytes 3538952 | tf_op jit(solution)/shard_map/ppermute | solution.py:70
  218.8 69.1 %all-to-all-start.3 = ((f32[8,16,784]{2,1,0:T(8,128)}), f32[8,16,784]{2,1,0:T(8,128)S(1)}, u32[]{:S(2)}, u32[]{:S(2)}) async-start(f32[8,16,784]{2,1,0:T(8,128)} %get-tuple-element.91), calls=%async_computation.3 | async-start | bytes 917504 | tf_op jit(solution)/shard_map/all_to_all | solution.py:846
  265.6 19.8 %collective-permute-start.61 = (f32[4,144,256]{2,1,0:T(8,128)S(1)}, f32[4,144,256]{2,1,0:T(8,128)S(1)}, u32[]{:S(2)}, u32[]{:S(2)}) collective-permute-start(f32[4,144,256]{2,1,0:T(8,128)S(1)} %pad_maximum_fusion.2), channel_id=1, source_target_pairs={{0,1},{1,0},{2,3},{3,2},{4,5},{5,4},{6,7},{7,6},{8,9},{9,8},{10,11... | collective-permute-start | bytes 1769480 | tf_op jit(solution)/shard_map/ppermute | solution.py:70
  268.2 58.9 %collective-permute-start.73 = (f32[16,128]{1,0:T(8,128)S(1)}, f32[16,128]{1,0:T(8,128)S(1)}, u32[]{:S(2)}, u32[]{:S(2)}) collective-permute-start(f32[16,128]{1,0:T(8,128)S(1)} %add.517), channel_id=1, source_target_pairs={{0,8},{1,9},{2,10},{3,11},{4,12},{5,13},{6,14},{7,15},{8,0},{9,1},... | collective-permute-start | bytes 24584 | tf_op jit(solution)/shard_map/ppermute | solution.py:70
  271.3 60.4 %collective-permute-start.59 = (f32[144,128]{1,0:T(8,128)S(1)}, f32[144,128]{1,0:T(8,128)S(1)}, u32[]{:S(2)}, u32[]{:S(2)}) collective-permute-start(f32[144,128]{1,0:T(8,128)S(1)} %add.490), channel_id=1, source_target_pairs={{0,8},{1,9},{2,10},{3,11},{4,12},{5,13},{6,14},{7,15},{8,0},{9,1},... | collective-permute-start | bytes 221192 | tf_op jit(solution)/shard_map/ppermute | solution.py:70
  287.9 59.1 %all-to-all-start.2 = ((f32[8,32,784]{2,1,0:T(8,128)}), f32[8,32,784]{2,1,0:T(8,128)S(1)}, u32[]{:S(2)}, u32[]{:S(2)}) async-start(f32[8,32,784]{2,1,0:T(8,128)} %shard_map.503), calls=%async_computation.2 | async-start | bytes 1835008 | tf_op jit(solution)/shard_map/all_to_all | solution.py:808
  294.5 20.3 %collective-permute-start.64 = (f32[144,256]{1,0:T(8,128)}, f32[144,256]{1,0:T(8,128)S(1)}, u32[]{:S(2)}, u32[]{:S(2)}) collective-permute-start(f32[144,256]{1,0:T(8,128)} %get-tuple-element.139), channel_id=1, source_target_pairs={{0,6},{1,7},{2,4},{3,5},{4,2},{5,3},{6,0},{7,1},{8,14},{9,15},{10,... | collective-permute-start | bytes 442376 | tf_op jit(solution)/shard_map/ppermute | solution.py:70
  299.0 26.5 %collective-permute-start.63 = (f32[144,256]{1,0:T(8,128)}, f32[144,256]{1,0:T(8,128)S(1)}, u32[]{:S(2)}, u32[]{:S(2)}) collective-permute-start(f32[144,256]{1,0:T(8,128)} %get-tuple-element.140), channel_id=1, source_target_pairs={{0,4},{1,5},{2,6},{3,7},{4,0},{5,1},{6,2},{7,3},{8,12},{9,13},{10,... | collective-permute-start | bytes 442376 | tf_op jit(solution)/shard_map/ppermute | solution.py:70
  309.6 18.1 %collective-permute-start.79 = (f32[144,256]{1,0:T(8,128)S(1)}, f32[144,256]{1,0:T(8,128)S(1)}, u32[]{:S(2)}, u32[]{:S(2)}) collective-permute-start(f32[144,256]{1,0:T(8,128)S(1)} %fusion.9), channel_id=1, source_target_pairs={{0,16},{1,17},{2,18},{3,19},{4,20},{5,21},{6,22},{7,23},{8,24},{9,... | collective-permute-start | bytes 442376 | tf_op jit(solution)/shard_map/ppermute | solution.py:70
  (139 other events, 1146.9 us)
